TPU v7x, 256 devices: a whole 4x4x8 slice. The times are simulated.
256 devices in a mesh: dp: 32 (over z, y), expert: 8 (over x, core).
Axes of the slice: x: 4, y: 4, z: 8, core: 2. Of those that a mesh axis runs over, the one named last changes fastest.
Arguments:
- tokens: bfloat16 [128, 32, 2048], P('dp'), may hold values from -20 to 20
- memory: bfloat16 [128, 32, 2048], P('dp', None, 'expert'), may hold values from -128 to 128
- source_length: int32 [128], P('dp'), may hold values from 1 to 32, 3072 in all
- owner_device: int32 [128], P('dp'), may hold values from 0 to 31, as said below
- source_device: int32 [128], P('dp'), may hold values from 0 to 31, as said below
- target_length: int32 [128], P('dp'), may hold values from 1 to 32, 3072 in all
- routing: int32 [128, 32, 2], P('dp'), may hold values from 0 to 31, all different within a row; in each aligned block of 128 rows (0 to 127, 128 to 255, ..., all dimensions but the last counted through in order) at most 16 rows name the same one
- attn_gain: float32 [2048], replicated, may hold values from 0.5 to 1.5
- ffn_gain: float32 [2048], replicated, may hold values from 0.5 to 1.5
- query_weight: bfloat16 [2048, 1024], P(None, 'expert'), may hold values from -1 to 1
- key_weight: bfloat16 [2048, 1024], P(None, 'expert'), may hold values from -1 to 1
- value_weight: bfloat16 [2048, 1024], P(None, 'expert'), may hold values from -0.125 to 0.125
- out_weight: bfloat16 [1024, 2048], P('expert'), may hold values from -0.1875 to 0.1875
- router_weight: bfloat16 [2048, 32], replicated, may hold values from -1 to 1
- up_weight: bfloat16 [32, 2048, 4096], P('dp', None, 'expert'), may hold values from -0.125 to 0.125
- down_weight: bfloat16 [32, 4096, 2048], P('dp', 'expert'), may hold values from -0.09375 to 0.09375
- grad_out: bfloat16 [128, 32, 2048], P('dp'), may hold values from -6 to 6
Outputs:
- memory_grad: bfloat16 [128, 32, 2048], P('dp', None, 'expert')
- up_grad: bfloat16 [32, 2048, 4096], P('dp', None, 'expert')
- down_grad: bfloat16 [32, 4096, 2048], P('dp', 'expert')
Inputs may be any that keep to these rules, and one draw needn't show every extreme that they name: Source sentence k of dp index i goes to position k of dp index owner_device[i * 4 + k]; for every k the sentences in position k of all dp indices go to all dp indices, one to each; one dp index sends at most one sentence to any other dp index. The inverse of owner_device: target position k of dp index j holds source sentence k of dp index source_device[j * 4 + k]. `routing`: among the 128 tokens of one dp index, at most 16 (token, choice) pairs name the same expert.
All inputs are finite; a program needn't handle non-finite values. No bound on the sum of `source_length` or of `target_length` on one device may be relied on, other than what follows from the above.
Results may differ from a plain program's by a relative error of at most 0.035.
The roundings to bfloat16 on the way count: a program that leaves them out, or rounds other values in their place, can miss the bound.
Values may be sent and summed in bfloat16 or wider, within the bound.
A program may use at most 64 MiB of HBM per device.

v0:
```python
import jax
import jax.numpy as jnp
from jax import lax
from jax.sharding import PartitionSpec as P

HEAD_DIM = 128


def layer_norm(values, norm_gain):
    average = jnp.mean(values, axis=-1, keepdims=True)
    centered = values - average
    variance = jnp.mean(centered * centered, axis=-1, keepdims=True)
    return centered * lax.rsqrt(variance + 1e-05) * norm_gain


def gate_from_logits(logits, routing_rows):
    chances = jax.nn.softmax(logits, axis=-1)
    chosen = (
        routing_rows[:, :, None] == jnp.arange(logits.shape[1], dtype=jnp.int32)[None, None, :]
    ).astype(jnp.float32)
    picked = jnp.einsum("rce,re->rc", chosen, chances, precision=lax.Precision.HIGHEST)
    return picked / jnp.sum(picked, axis=-1, keepdims=True)


def router_back(logit_grad, router_weight):
    high_part = logit_grad.astype(jnp.bfloat16)
    low_part = (logit_grad - high_part.astype(jnp.float32)).astype(jnp.bfloat16)
    return jnp.einsum(
        "re,de->rd", high_part, router_weight, preferred_element_type=jnp.float32
    ) + jnp.einsum("re,de->rd", low_part, router_weight, preferred_element_type=jnp.float32)


def slot_ranks(routing_rows, expert_count):
    pair_expert = routing_rows.reshape(-1)
    matches = (pair_expert[:, None] == jnp.arange(expert_count, dtype=jnp.int32)[None, :]).astype(
        jnp.int32
    )
    ranked = jnp.sum(jnp.cumsum(matches, axis=0) * matches, axis=1) - 1
    return ranked.reshape(routing_rows.shape)


def attend(queries, key_heads, value_heads, key_length):
    scaling = queries.shape[-1] ** (-0.5)
    scores = (
        jnp.einsum("sqhd,skhd->shqk", queries, key_heads, preferred_element_type=jnp.float32)
        * scaling
    )
    key_open = jnp.arange(key_heads.shape[1], dtype=jnp.int32)[None, :] < key_length[:, None]
    scores = jnp.where(key_open[:, None, None, :], scores, -1e30)
    probabilities = jax.nn.softmax(scores, axis=-1)
    weights = probabilities.astype(jnp.bfloat16)
    attended = jnp.einsum(
        "shqk,skhd->sqhd", weights, value_heads, preferred_element_type=jnp.float32
    ).astype(jnp.bfloat16)
    return (attended, probabilities, weights)


def attend_back(queries, value_heads, probabilities, weights, attended_grad):
    scaling = queries.shape[-1] ** (-0.5)
    value_grad = jnp.einsum(
        "shqk,sqhd->skhd", weights, attended_grad, preferred_element_type=jnp.float32
    ).astype(jnp.bfloat16)
    prob_grad = jnp.einsum(
        "sqhd,skhd->shqk", attended_grad, value_heads, preferred_element_type=jnp.float32
    )
    score_grad = (
        probabilities
        * (prob_grad - jnp.sum(probabilities * prob_grad, axis=-1, keepdims=True))
        * scaling
    ).astype(jnp.bfloat16)
    key_grad = jnp.einsum(
        "shqk,sqhd->skhd", score_grad, queries, preferred_element_type=jnp.float32
    ).astype(jnp.bfloat16)
    return (key_grad, value_grad)


def body(
    tokens,
    memory,
    source_length,
    owner_device,
    source_device,
    target_length,
    routing,
    attn_gain,
    ffn_gain,
    query_weight,
    key_weight,
    value_weight,
    out_weight,
    router_weight,
    up_weight,
    down_weight,
    grad_out,
):
    dp_count = lax.axis_size("dp")
    slice_count = lax.axis_size("expert")
    sentence_count, target_len, model_width = tokens.shape
    source_len = memory.shape[1]
    slice_width = memory.shape[2]
    slot_count = (sentence_count + dp_count - 1) // dp_count
    slot_rows = dp_count * slot_count
    position = jnp.arange(sentence_count, dtype=jnp.int32)
    slot_index = jnp.arange(slot_rows, dtype=jnp.int32)
    send_plan = (
        slot_index[:, None] == (owner_device * slot_count + position // dp_count)[None, :]
    ).astype(jnp.bfloat16)
    take_plan = (
        (source_device * slot_count + position // dp_count)[:, None] == slot_index[None, :]
    ).astype(jnp.bfloat16)
    outbound = jnp.dot(
        send_plan,
        memory.reshape(sentence_count, source_len * slice_width),
        preferred_element_type=jnp.float32,
    ).astype(jnp.bfloat16)
    outbound_len = jnp.dot(
        send_plan, source_length.astype(jnp.bfloat16)[:, None], preferred_element_type=jnp.float32
    ).astype(jnp.bfloat16)
    inbound, inbound_len = (
        lax.all_to_all(outbound, "dp", split_axis=0, concat_axis=0, tiled=True),
        lax.all_to_all(outbound_len, "dp", split_axis=0, concat_axis=0, tiled=True),
    )
    arrived = (
        jnp.dot(take_plan, inbound, preferred_element_type=jnp.float32)
        .astype(jnp.bfloat16)
        .reshape(sentence_count * source_len, slice_width)
    )
    key_length = jnp.dot(take_plan, inbound_len, preferred_element_type=jnp.float32)[:, 0].astype(
        jnp.int32
    )
    head_cols = key_weight.shape[1]
    heads_here = head_cols // HEAD_DIM
    portion = lax.all_gather(arrived, "expert", axis=1, tiled=True)
    key_acc = jnp.dot(portion, key_weight, preferred_element_type=jnp.float32)
    value_acc = jnp.dot(portion, value_weight, preferred_element_type=jnp.float32)
    key_heads = key_acc.astype(jnp.bfloat16).reshape(
        sentence_count, source_len, heads_here, HEAD_DIM
    )
    value_heads = value_acc.astype(jnp.bfloat16).reshape(
        sentence_count, source_len, heads_here, HEAD_DIM
    )
    token_rows = sentence_count * target_len
    flat_tokens = tokens.reshape(token_rows, model_width)
    normed = layer_norm(flat_tokens.astype(jnp.float32), attn_gain).astype(jnp.bfloat16)
    queries = (
        jnp.dot(normed, query_weight, preferred_element_type=jnp.float32)
        .astype(jnp.bfloat16)
        .reshape(sentence_count, target_len, heads_here, HEAD_DIM)
    )
    attended, probabilities, weights = attend(queries, key_heads, value_heads, key_length)
    partial_value = jnp.dot(
        attended.reshape(token_rows, head_cols), out_weight, preferred_element_type=jnp.float32
    )
    hidden = (
        flat_tokens.astype(jnp.float32)
        + lax.psum(partial_value.astype(jnp.bfloat16), "expert").astype(jnp.float32)
    ).astype(jnp.bfloat16)
    expert_in = layer_norm(hidden.astype(jnp.float32), ffn_gain).astype(jnp.bfloat16)
    routing_rows = routing.reshape(token_rows, 2)
    logits = jnp.dot(expert_in, router_weight, preferred_element_type=jnp.float32)
    gate_shares = gate_from_logits(logits, routing_rows)
    capacity = slice_count * ((3 * token_rows // dp_count + slice_count - 1) // slice_count)
    slot_rank = slot_ranks(routing_rows, dp_count)
    slot_id = routing_rows * capacity + slot_rank
    pair_plans = (
        slot_id[:, :, None] == jnp.arange(dp_count * capacity, dtype=jnp.int32)[None, None, :]
    ).astype(jnp.bfloat16)
    pair_plan = pair_plans[:, 0] + pair_plans[:, 1]

    def send_slots(builder):
        arrived_slots = lax.all_to_all(
            builder(0, capacity), "dp", split_axis=0, concat_axis=0, tiled=True
        )
        return arrived_slots.reshape(dp_count * capacity, model_width)

    def reduce_slices(addend_blocks):
        widened = lax.optimization_barrier(addend_blocks).astype(jnp.float32)
        return lax.psum_scatter(
            widened.astype(jnp.bfloat16), "expert", scatter_dimension=1, tiled=True
        )

    def sum_slices(partial_rows):
        blocks = partial_rows.reshape(dp_count, capacity, model_width)
        returned = lax.all_to_all(blocks, "dp", split_axis=0, concat_axis=0, tiled=True)
        summed = reduce_slices(returned)
        filled = lax.all_gather(summed, "expert", axis=1, tiled=True)
        return filled.reshape(dp_count * capacity, model_width)

    def build_inputs(offset, span_rows):
        sub_plan = pair_plan.reshape(token_rows, dp_count, capacity)
        return jnp.einsum(
            "rec,rd->ecd", sub_plan, expert_in, preferred_element_type=jnp.float32
        ).astype(jnp.bfloat16)

    up_slice = up_weight[0]
    down_slice = down_weight[0]
    slots_in = send_slots(build_inputs)
    pre_act = jnp.dot(slots_in, up_slice, preferred_element_type=jnp.float32)
    activation = jax.nn.gelu(pre_act).astype(jnp.bfloat16)
    expert_out = sum_slices(
        jnp.dot(activation, down_slice, preferred_element_type=jnp.float32).astype(jnp.bfloat16)
    )
    target_live = jnp.arange(target_len, dtype=jnp.int32)[None, :] < target_length[:, None]
    live_grad = jnp.where(target_live[:, :, None], grad_out, jnp.zeros((), jnp.bfloat16)).reshape(
        token_rows, model_width
    )
    grad_slots = jnp.einsum("rq,rd->qd", pair_plan, live_grad, preferred_element_type=jnp.float32)
    slot_gate = jnp.einsum(
        "rc,rcq->q", gate_shares, pair_plans.astype(jnp.float32), precision=lax.Precision.HIGHEST
    )
    slot_gate_grad = jnp.sum(expert_out.astype(jnp.float32) * grad_slots, axis=-1)
    gate_grad = jnp.einsum(
        "rcq,q->rc", pair_plans.astype(jnp.float32), slot_gate_grad, precision=lax.Precision.HIGHEST
    )
    scaled_grad = (
        (grad_slots * slot_gate[:, None])
        .astype(jnp.bfloat16)
        .reshape(dp_count, capacity, model_width)
    )

    def build_grads(offset, span_rows):
        return scaled_grad

    out_grad = send_slots(build_grads)
    down_grad = jnp.einsum(
        "rf,rd->fd", activation, out_grad, preferred_element_type=jnp.float32
    ).astype(jnp.bfloat16)
    act_grad = jnp.einsum("rd,fd->rf", out_grad, down_slice, preferred_element_type=jnp.float32)
    pre_grad = jax.vjp(jax.nn.gelu, pre_act)[1](act_grad)[0].astype(jnp.bfloat16)
    up_grad = jnp.einsum(
        "rd,rf->df", slots_in, pre_grad, preferred_element_type=jnp.float32
    ).astype(jnp.bfloat16)
    input_slots = sum_slices(
        jnp.einsum("rf,df->rd", pre_grad, up_slice, preferred_element_type=jnp.float32).astype(
            jnp.bfloat16
        )
    )
    input_pairs = jnp.einsum(
        "rcq,qd->rcd", pair_plans, input_slots, preferred_element_type=jnp.float32
    )
    ffn_in_grad = jnp.sum(gate_shares[:, :, None] * input_pairs, axis=1)
    logit_grad = jax.vjp(lambda inputs: gate_from_logits(inputs, routing_rows), logits)[1](
        gate_grad
    )[0]
    ffn_in_grad = ffn_in_grad + router_back(logit_grad, router_weight)
    norm_back = jax.vjp(lambda inputs: layer_norm(inputs, ffn_gain), hidden.astype(jnp.float32))[1]
    hidden_grad = (live_grad.astype(jnp.float32) + norm_back(ffn_in_grad)[0]).astype(jnp.bfloat16)
    attended_grad = jnp.einsum(
        "rd,cd->rc", hidden_grad, out_weight, preferred_element_type=jnp.float32
    ).astype(jnp.bfloat16)
    attended_grad = attended_grad.reshape(sentence_count, target_len, heads_here, HEAD_DIM)
    key_grad, value_grad = attend_back(queries, value_heads, probabilities, weights, attended_grad)
    memory_part = jnp.einsum(
        "rc,dc->rd",
        key_grad.reshape(sentence_count * source_len, head_cols),
        key_weight,
        preferred_element_type=jnp.float32,
    )
    memory_part = memory_part + jnp.einsum(
        "rc,dc->rd",
        value_grad.reshape(sentence_count * source_len, head_cols),
        value_weight,
        preferred_element_type=jnp.float32,
    )
    memory_share = lax.psum_scatter(
        memory_part.astype(jnp.bfloat16), "expert", scatter_dimension=1, tiled=True
    )
    homeward = jnp.einsum(
        "sq,sx->qx",
        take_plan,
        memory_share.reshape(sentence_count, source_len * slice_width),
        preferred_element_type=jnp.float32,
    ).astype(jnp.bfloat16)
    homecoming = lax.all_to_all(homeward, "dp", split_axis=0, concat_axis=0, tiled=True)
    memory_grad = jnp.einsum(
        "qs,qx->sx", send_plan, homecoming, preferred_element_type=jnp.float32
    ).astype(jnp.bfloat16)
    return (
        memory_grad.reshape(sentence_count, source_len, slice_width),
        up_grad[None],
        down_grad[None],
    )


def solution(mesh):
    in_specs = (
        P("dp", None, None),
        P("dp", None, "expert"),
        P("dp"),
        P("dp"),
        P("dp"),
        P("dp"),
        P("dp", None, None),
        P(),
        P(),
        P(None, "expert"),
        P(None, "expert"),
        P(None, "expert"),
        P("expert", None),
        P(),
        P("dp", None, "expert"),
        P("dp", "expert", None),
        P("dp", None, None),
    )
    out_specs = (P("dp", None, "expert"), P("dp", None, "expert"), P("dp", "expert", None))
    return jax.shard_map(body, mesh=mesh, in_specs=in_specs, out_specs=out_specs, check_vma=False)
```

profile of v0, /device:TPU:1, one launch (start us, length us, event | category | flops | bytes accessed | tf_op | source)
XLA Modules:
  0.0 599.4 jit_solution(3185587439850993753)
XLA Ops:
  9.5 12.0 %all-to-all-start = ((bf16[32,1,1]{2,1,0:T(2,128)(2,1)}), bf16[32,1,1]{2,1,0:T(2,128)(2,1)S(1)}, u32[]{:S(2)}, u32[]{:S(2)}) async-start(bf16[32,1,1]{2,1,0:T(2,128)(2,1)} %copy.61), calls=%async_computation | async-start | bytes 32768 | tf_op jit(solution)/shard_map/all_to_all | solution.py:121
  29.2 2.7 reduce.15
  34.1 9.3 %all-to-all-start.1 = ((bf16[32,2,4096]{2,1,0:T(2,128)(2,1)}), bf16[32,2,4096]{2,1,0:T(2,128)(2,1)}, u32[]{:S(2)}, u32[]{:S(2)}) async-start(bf16[32,2,4096]{2,1,0:T(2,128)(2,1)} %reshape.344), calls=%async_computation.1 | async-start | bytes 1048576 | tf_op jit(solution)/shard_map/all_to_all | solution.py:120
  45.8 13.0 %all-to-all-done.1 = bf16[32,2,4096]{2,1,0:T(2,128)(2,1)} async-done(((bf16[32,2,4096]{2,1,0:T(2,128)(2,1)}), bf16[32,2,4096]{2,1,0:T(2,128)(2,1)}, u32[]{:S(2)}, u32[]{:S(2)}) %all-to-all-start.1) | async-done | bytes 524320 | tf_op jit(solution)/shard_map/all_to_all | solution.py:120
  58.8 4.4 reshape.345
  65.2 16.7 %all_gather.9 = bf16[128,2048]{1,0:T(8,128)(2,1)S(1)} all-gather(bf16[128,256]{1,0:T(8,128)(2,1)S(1)} %reshape.308), channel_id=1, replica_groups=mesh['dp'=32,'expert'=8] {'expert'}, dimensions={1}, use_global_device_ids=true | all-gather | bytes 589824 | tf_op jit(solution)/shard_map/all_gather | solution.py:133
  87.3 58.6 %all-reduce.2.cloned.1.call-done = bf16[128,2048]{1,0:T(8,128)(2,1)} async-done(((bf16[128,2048]{1,0:T(8,128)(2,1)}), bf16[128,2048]{1,0:T(8,128)(2,1)}) %all-reduce.2.cloned.1.call-update) | async-done | bytes 524304 | tf_op jit(solution)/shard_map/psum | solution.py:156
  148.3 56.5 %all_to_all.53 = bf16[32,16,2048]{2,1,0:T(8,128)(2,1)S(1)} all-to-all(bf16[32,16,2048]{2,1,0:T(8,128)(2,1)S(1)} %convolution_convert_fusion.4), channel_id=1, replica_groups=mesh['dp'=32,'expert'=8] {'dp'}, dimensions={0} | all-to-all | bytes 4194304 | tf_op jit(solution)/shard_map/all_to_all | solution.py:171
  208.8 53.0 %all_to_all.54 = bf16[32,16,2048]{2,1,0:T(8,128)(2,1)S(1)} all-to-all(bf16[32,16,2048]{2,1,0:T(8,128)(2,1)S(1)} %bitcast.180), channel_id=1, replica_groups=mesh['dp'=32,'expert'=8] {'dp'}, dimensions={0} | all-to-all | bytes 4194304 | tf_op jit(solution)/shard_map/all_to_all | solution.py:184
  261.8 2.5 copy.73
  264.4 37.6 %reduce-scatter.6.cloned.1.call-done = bf16[32,2,2048]{2,0,1:T(8,128)(2,1)} async-done(((bf16[32,16,2048]{2,0,1:T(8,128)(2,1)}), bf16[32,2,2048]{2,0,1:T(8,128)(2,1)}) %reduce-scatter.6.cloned.1.call-update) | async-done | bytes 262160 | tf_op jit(solution)/shard_map/reduce_scatter | solution.py:178
  309.2 24.4 %all-gather.5.cloned.1.call-done = bf16[32,16,2048]{2,0,1:T(8,128)(2,1)} async-done(((bf16[32,2,2048]{2,0,1:T(8,128)(2,1)}), bf16[32,16,2048]{2,0,1:T(8,128)(2,1)}) %all-gather.5.cloned.1.call-update) | async-done | bytes 2097168 | tf_op jit(solution)/shard_map/all_gather | solution.py:186
  333.6 2.8 copy.74
  337.2 58.9 %all_to_all.55 = bf16[32,16,2048]{2,1,0:T(8,128)(2,1)S(1)} all-to-all(bf16[32,16,2048]{2,1,0:T(8,128)(2,1)S(1)} %bitcast.172), channel_id=1, replica_groups=mesh['dp'=32,'expert'=8] {'dp'}, dimensions={0} | all-to-all | bytes 4194304 | tf_op jit(solution)/shard_map/all_to_all | solution.py:171
  400.5 54.0 %all_to_all.56 = bf16[32,16,2048]{2,1,0:T(8,128)(2,1)S(1)} all-to-all(bf16[32,16,2048]{2,1,0:T(8,128)(2,1)S(1)} %bitcast.181), channel_id=1, replica_groups=mesh['dp'=32,'expert'=8] {'dp'}, dimensions={0} | all-to-all | bytes 4194304 | tf_op jit(solution)/shard_map/all_to_all | solution.py:184
  457.1 32.1 %reduce-scatter.4.cloned.1.call-done = bf16[32,2,2048]{2,0,1:T(8,128)(2,1)} async-done(((bf16[32,16,2048]{2,0,1:T(8,128)(2,1)}), bf16[32,2,2048]{2,0,1:T(8,128)(2,1)}) %reduce-scatter.4.cloned.1.call-update) | async-done | bytes 262160 | tf_op jit(solution)/shard_map/reduce_scatter | solution.py:178
  491.6 29.0 %all-gather.3.cloned.1.call-done = bf16[32,16,2048]{2,0,1:T(8,128)(2,1)} async-done(((bf16[32,2,2048]{2,0,1:T(8,128)(2,1)}), bf16[32,16,2048]{2,0,1:T(8,128)(2,1)}) %all-gather.3.cloned.1.call-update) | async-done | bytes 2097168 | tf_op jit(solution)/shard_map/all_gather | solution.py:186
  520.7 2.7 copy.71
  530.2 31.2 %reduce-scatter.8.cloned.1.call-done = bf16[128,256]{1,0:T(8,128)(2,1)} async-done(((bf16[128,2048]{1,0:T(8,128)(2,1)}), bf16[128,256]{1,0:T(8,128)(2,1)}) %reduce-scatter.8.cloned.1.call-update) | async-done | bytes 65552 | tf_op jit(solution)/shard_map/reduce_scatter | solution.py:265
  564.9 9.4 %all-to-all-start.6 = ((bf16[32,2,4096]{2,1,0:T(2,128)(2,1)}), bf16[32,2,4096]{2,1,0:T(2,128)(2,1)}, u32[]{:S(2)}, u32[]{:S(2)}) async-start(bf16[32,2,4096]{2,1,0:T(2,128)(2,1)} %reshape.346), calls=%async_computation.9 | async-start | bytes 1048576 | tf_op jit(solution)/shard_map/all_to_all | solution.py:274
  574.4 4.4 fusion.5
  578.7 2.7 fusion.6
  581.5 6.1 %all-to-all-done.6 = bf16[32,2,4096]{2,1,0:T(2,128)(2,1)} async-done(((bf16[32,2,4096]{2,1,0:T(2,128)(2,1)}), bf16[32,2,4096]{2,1,0:T(2,128)(2,1)}, u32[]{:S(2)}, u32[]{:S(2)}) %all-to-all-start.6) | async-done | bytes 524320 | tf_op jit(solution)/shard_map/all_to_all | solution.py:274
  587.6 3.6 reshape.347
  (218 shorter events, 56.8 us)
Async XLA Ops:
  7.2 200.3 %copy-start = (bf16[1,512,2048]{2,1,0:T(8,128)(2,1)S(1)}, bf16[1,512,2048]{2,1,0:T(8,128)(2,1)}, u32[]{:S(2)}) copy-start(bf16[1,512,2048]{2,1,0:T(8,128)(2,1)} %param.32) | copy-start | bytes 6291460
  9.5 24.6 %all-to-all-start = ((bf16[32,1,1]{2,1,0:T(2,128)(2,1)}), bf16[32,1,1]{2,1,0:T(2,128)(2,1)S(1)}, u32[]{:S(2)}, u32[]{:S(2)}) async-start(bf16[32,1,1]{2,1,0:T(2,128)(2,1)} %copy.61), calls=%async_computation | async-start | bytes 32768 | tf_op jit(solution)/shard_map/all_to_all | solution.py:121
  34.1 24.7 %all-to-all-start.1 = ((bf16[32,2,4096]{2,1,0:T(2,128)(2,1)}), bf16[32,2,4096]{2,1,0:T(2,128)(2,1)}, u32[]{:S(2)}, u32[]{:S(2)}) async-start(bf16[32,2,4096]{2,1,0:T(2,128)(2,1)} %reshape.344), calls=%async_computation.1 | async-start | bytes 1048576 | tf_op jit(solution)/shard_map/all_to_all | solution.py:120
  43.5 102.4 %all-reduce.2.cloned.1.call-start = ((), (), s32[]{:S(2)}) async-start(), calls=%async_computation.10 | async-start | bytes 1048576 | tf_op jit(solution)/shard_map/psum | solution.py:156
  43.5 38.4 %copy-start.36 = (s32[4]{0:T(128)}, s32[4]{0:T(128)S(1)}, u32[]{:S(2)}) copy-start(s32[4]{0:T(128)S(1)} %fusion.88) | copy-start | bytes 52
  43.8 43.3 %copy-start.30 = (s32[128,2]{0,1:T(2,128)}, s32[128,2]{0,1:T(2,128)S(1)}, u32[]{:S(2)}) copy-start(s32[128,2]{0,1:T(2,128)S(1)} %multiply_add_fusion) | copy-start | bytes 3076
  45.2 39.1 %copy-start.17 = (bf16[128,128]{1,0:T(8,128)(2,1)}, bf16[128,128]{1,0:T(8,128)(2,1)S(1)}, u32[]{:S(2)}) copy-start(bf16[128,128]{1,0:T(8,128)(2,1)S(1)} %convolution_convert_fusion.15) | copy-start | bytes 98308
  45.2 38.0 %copy-start.3 = (bf16[2048,128]{1,0:T(8,128)(2,1)S(1)}, bf16[2048,128]{1,0:T(8,128)(2,1)}, u32[]{:S(2)}) copy-start(bf16[2048,128]{1,0:T(8,128)(2,1)} %param.27) | copy-start | bytes 1572868
  45.8 38.5 %copy-start.46 = (pred[4,32]{1,0:T(4,128)(4,1)}, pred[4,32]{1,0:T(4,128)(4,1)S(1)}, u32[]{:S(2)}) copy-start(pred[4,32]{1,0:T(4,128)(4,1)S(1)} %iota_compare_fusion.11) | copy-start | bytes 388
  84.9 62.6 %copy-start.15 = (f32[2048]{0:T(1024)S(1)}, f32[2048]{0:T(1024)}, u32[]{:S(2)}) copy-start(f32[2048]{0:T(1024)} %param.25) | copy-start | bytes 24580
  87.1 214.9 %reduce-scatter.6.cloned.1.call-start = ((), (), s32[]{:S(2)}) async-start(), calls=%async_computation.13 | async-start | bytes 2359296 | tf_op jit(solution)/shard_map/reduce_scatter | solution.py:178
  147.2 156.2 %copy-start.27 = (f32[128]{0:T(128)}, f32[128]{0:T(128)S(1)}, u32[]{:S(2)}) copy-start(f32[128]{0:T(128)S(1)} %broadcast_multiply_fusion.1) | copy-start | bytes 1540
  147.5 57.4 %copy-start.40 = (f32[128]{0:T(128)}, f32[128]{0:T(128)S(1)}, u32[]{:S(2)}) copy-start(f32[128]{0:T(128)S(1)} %fusion.33) | copy-start | bytes 1540
  147.5 155.9 %copy-start.32 = (f32[128]{0:T(128)}, f32[128]{0:T(128)S(1)}, u32[]{:S(2)}) copy-start(f32[128]{0:T(128)S(1)} %fusion.90) | copy-start | bytes 1540
  148.3 57.9 %copy-start.42 = (bf16[1,2048,512]{2,1,0:T(8,128)(2,1)S(1)}, bf16[1,2048,512]{2,1,0:T(8,128)(2,1)}, u32[]{:S(2)}) copy-start(bf16[1,2048,512]{2,1,0:T(8,128)(2,1)} %param.31) | copy-start | bytes 6291460
  264.3 37.8 %copy-start.45 = (s32[4]{0:T(128)S(1)}, s32[4]{0:T(128)}, u32[]{:S(2)}) copy-start(s32[4]{0:T(128)} %param.22) | copy-start | bytes 52
  264.3 39.1 %copy-start.11 = (bf16[2048,32]{0,1:T(8,128)(2,1)S(1)}, bf16[2048,32]{0,1:T(8,128)(2,1)}, u32[]{:S(2)}) copy-start(bf16[2048,32]{0,1:T(8,128)(2,1)} %param.30) | copy-start | bytes 393220
  264.3 69.2 %all-gather.5.cloned.1.call-start = ((), (), s32[]{:S(2)}) async-start(), calls=%async_computation.14 | async-start | bytes 2359296 | tf_op jit(solution)/shard_map/all_gather | solution.py:186
  302.0 187.1 %reduce-scatter.4.cloned.1.call-start = ((), (), s32[]{:S(2)}) async-start(), calls=%async_computation.11 | async-start | bytes 2359296 | tf_op jit(solution)/shard_map/reduce_scatter | solution.py:178
  337.2 60.2 %copy-start.51 = (f32[512,512]{1,0:T(8,128)S(1)}, f32[512,512]{1,0:T(8,128)}, u32[]{:S(2)}) copy-start(f32[512,512]{1,0:T(8,128)} %copy-done.50) | copy-start | bytes 3145732
  457.0 63.7 %all-gather.3.cloned.1.call-start = ((), (), s32[]{:S(2)}) async-start(), calls=%async_computation.12 | async-start | bytes 2359296 | tf_op jit(solution)/shard_map/all_gather | solution.py:186
  489.2 72.2 %reduce-scatter.8.cloned.1.call-start = ((), (), s32[]{:S(2)}) async-start(), calls=%async_computation.15 | async-start | bytes 589824 | tf_op jit(solution)/shard_map/reduce_scatter | solution.py:265
  528.8 33.5 %copy-start.37 = (s32[4]{0:T(128)S(1)}, s32[4]{0:T(128)}, u32[]{:S(2)}) copy-start(s32[4]{0:T(128)} %copy-done.36) | copy-start | bytes 52
  564.9 22.7 %all-to-all-start.6 = ((bf16[32,2,4096]{2,1,0:T(2,128)(2,1)}), bf16[32,2,4096]{2,1,0:T(2,128)(2,1)}, u32[]{:S(2)}, u32[]{:S(2)}) async-start(bf16[32,2,4096]{2,1,0:T(2,128)(2,1)} %reshape.346), calls=%async_computation.9 | async-start | bytes 1048576 | tf_op jit(solution)/shard_map/all_to_all | solution.py:274
  (40 other events, 419.4 us)
Sparse Core Ops, SparseCore 0:
  87.2 58.6 all-reduce.1
  264.5 37.4 reduce-scatter.5
  304.0 29.5 all-gather.4
  457.1 31.9 reduce-scatter.3
  491.0 29.6 all-gather.2
  530.3 30.9 reduce-scatter.7
where the time goes:
time: 605 us; the launch traced here: 599 us
  blocking collectives  239 us (40%)
  waiting for transfers between devices  232 us (38%)
  matrix products  34 us (6%)
  local copies, waits for them, and re-layouts  33.2 us (5%)
  starting transfers between devices  31.3 us (5%)
  other arithmetic  14.9 us (2%)
  between operations  14.9 us (2%)
    all_to_all x2, blocking collectives, send_slots(): lax.all_to_all(builder(0, capacity), 'dp', split_axis=0, concat_axis=0, t...  115 us
    all_to_all x2, blocking collectives, sum_slices(): lax.all_to_all(blocks, 'dp', split_axis=0, concat_axis=0, tiled=True)  107 us
    reduce_scatter x2, waiting for transfers between devices, reduce_slices(): lax.psum_scatter(widened.astype(jnp.bfloat16), 'expert', scatter_dimensio...  69.6 us
    psum x1, waiting for transfers between devices, body(): lax.psum(partial_value.astype(jnp.bfloat16), 'expert').astype(jnp.float32)  58.6 us
    all_gather x2, waiting for transfers between devices, sum_slices(): filled = lax.all_gather(summed, 'expert', axis=1, tiled=True)  53.4 us
    reduce_scatter x1, waiting for transfers between devices, body(): lax.psum_scatter(memory_part.astype(jnp.bfloat16), 'expert', scatter_dime...  31.2 us
    unnamed x120, local copies, waits for them, and re-layouts  18.8 us
    all_gather x1, blocking collectives, body(): portion = lax.all_gather(arrived, 'expert', axis=1, tiled=True)  16.7 us
  transfers between devices with their start and end apart: 9, of which 8 were waited for; matrix products, arithmetic and copies ran while one was open for 5% of the time, Pallas kernels for 0%

commit v1 on v0

v1 whole, which is shorter than its diff:
```python
import functools

import jax
import jax.numpy as jnp
from jax import lax
from jax.experimental import pallas as pl
from jax.experimental.pallas import tpu as pltpu
from jax.sharding import PartitionSpec as P

F32 = jnp.float32
BF16 = jnp.bfloat16
HI = lax.Precision.HIGHEST
LANES = 128
CAP = 16
TILE = 16
GROUPS = 4
EPS = 1e-5


def dot(a, b, ca=1, cb=0, precision=None):
    return lax.dot_general(
        a, b, (((ca,), (cb,)), ((), ())), preferred_element_type=F32, precision=precision
    )


def iota(shape, dim):
    return lax.broadcasted_iota(jnp.int32, shape, dim)


def log2(value):
    return value.bit_length() - 1


def to_rows(columns):
    rows = columns[0].shape[0]
    lane = iota((rows, LANES), 1)
    packed = jnp.zeros((rows, LANES), F32)
    for i, column in enumerate(columns):
        packed = jnp.where(lane == i, column, packed)
    return packed.T[:8]


def to_columns(rows, count):
    padded = jnp.concatenate([rows, jnp.zeros((LANES - 8, rows.shape[1]), F32)], axis=0).T
    return [padded[:, i : i + 1] for i in range(count)]


def stack_rows(*rows):
    fill = jnp.zeros((8 - len(rows), rows[0].shape[1]), F32)
    return jnp.concatenate([*rows, fill], axis=0)


class Layout:
    def __init__(self, n_dp, n_e, sentences, length, width, head, hidden, experts):
        self.n_dp, self.n_e, self.n_x = n_dp, n_e, n_e // 2
        self.S, self.L, self.T = sentences, length, sentences * length
        self.D, self.F = width, width // n_e
        self.Hd, self.H, self.E = head, hidden, experts
        self.R = n_dp * CAP
        self.mids = n_dp // 2
        self.gs = n_dp // GROUPS
        self.Q = self.R // GROUPS


def layer_kernel(
    z,
    src_ref, slen_ref, tlen_ref, routing_ref, again_ref, fgain_ref,
    tokens_hbm, memory_hbm, grad_hbm, wq_hbm, wk_hbm, wv_hbm, wo_hbm, wr_hbm, up_hbm, down_hbm,
    mem_out, up_out, down_out,
    tok, live, wq, wk, wv, wo, wr, up, down,
    mem_all, ow_all, att_all, hg_all, x_all, g_all,
    g_send, x_send, ret_send, ret_recv,
    meta, kv_send, mid_buf, mid_out_buf, kv_recv, kvg_send, mid_buf2, mid_out2, kvg_recv,
    stat1, stat2, lg_all, gate_send, gate_recv, gg_all, gg_send, gg_recv,
    plan, plan0, plan1, relay_plan, u_buf, act_buf, pg_buf,
    sib_send, sib_recv, pair, xs_send, far_recv, lft_recv, rgt_recv,
    m_sib_send, m_sib_recv, m_pair, m_xs_send, m_far_recv, m_lft_recv, m_rgt_recv,
    ug, dg, mg, hid,
    ss, rs, ls,
):
    n_dp, n_e, T, D, F, R, Q = z.n_dp, z.n_e, z.T, z.D, z.F, z.R, z.Q
    me = lax.axis_index("dp")
    e = lax.axis_index("expert")
    x, c = e // 2, e % 2
    xr, xl = (x + 1) % 4, (x + 3) % 4
    sib = 2 * x + (1 - c)
    right, left = 2 * xr + c, 2 * xl + c
    my_group = me // z.gs
    col_e = pl.multiple_of(e * F, F)

    counter = [0]

    def sems(count):
        first = counter[0]
        counter[0] += count
        return first

    def copy(src, dst, k, dp, ex, ks=None):
        return pltpu.make_async_remote_copy(
            src_ref=src,
            dst_ref=dst,
            send_sem=ss.at[k if ks is None else ks],
            recv_sem=rs.at[k],
            device_id=(dp, ex),
            device_id_type=pl.DeviceIdType.MESH,
        )

    pending = []

    def send(src, dst, k, dp, ex):
        copy(src, dst, k, dp, ex).start()
        pending.append(lambda: copy(src, dst, k, dp, ex).wait_send())

    def arrive(dst, k):
        copy(dst, dst, k, me, sib).wait_recv()

    def rows16(ref, i):
        return ref.at[pl.ds(pl.multiple_of(i * CAP, CAP), CAP)]

    def one_row(ref, i):
        return ref.at[pl.ds(i, 1)]

    class Spread:
        def __init__(self, src, dst):
            self.src, self.dst = src, dst
            self.base = sems(n_dp)

        def one(self, t):
            return copy(self.src(t), self.dst(me), self.base + me, t, e, ks=self.base + t)

        def start(self):
            def step(kk, carry):
                group = (my_group + kk // z.gs) % GROUPS
                t = group * z.gs + (me % z.gs + kk % z.gs) % z.gs
                self.one(t).start()
                return carry

            lax.fori_loop(1, n_dp, step, 0)

            def finish():
                def step(kk, carry):
                    self.one((me + kk) % n_dp).wait_send()
                    return carry

                lax.fori_loop(1, n_dp, step, 0)

            pending.append(finish)

        def start_group(self, group):
            def step(kk, carry):
                t = group * z.gs + (me % z.gs + kk) % z.gs

                @pl.when(t != me)
                def _():
                    self.one(t).start()

                return carry

            lax.fori_loop(0, z.gs, step, 0)

        def finish_later(self):
            def finish():
                def step(kk, carry):
                    self.one((me + kk) % n_dp).wait_send()
                    return carry

                lax.fori_loop(1, n_dp, step, 0)

            pending.append(finish)

        def wait_group(self, group):
            def step(kk, carry):
                i = group * z.gs + kk

                @pl.when(i != me)
                def _():
                    arrive(self.dst(i), self.base + i)

                return carry

            lax.fori_loop(0, z.gs, step, 0)

        def wait(self):
            def step(kk, carry):
                i = (me + n_dp - kk) % n_dp
                arrive(self.dst(i), self.base + i)
                return carry

            lax.fori_loop(1, n_dp, step, 0)

    class Gather:
        def __init__(self, part, parts):
            self.part, self.parts = part, parts
            self.base = sems(7 * parts)

        def go(self, q, t, block, peer):
            ref = self.part(block, q)
            send(ref, ref, self.base + 7 * q + t, me, peer)

        def got(self, q, t, block):
            arrive(self.part(block, q), self.base + 7 * q + t)

        def start(self, q):
            self.go(q, 0, e, right)
            self.go(q, 1, e, left)
            self.go(q, 2, e, sib)

        def mid(self, q):
            self.got(q, 0, left)
            if q % 2 == 0:
                self.go(q, 6, left, right)
            self.go(q, 3, left, sib)
            self.got(q, 1, right)
            if q % 2 == 1:
                self.go(q, 6, right, left)
            self.go(q, 4, right, sib)

        def far(self, q):
            across = 2 * ((x + 2) % 4) + c
            self.got(q, 6, across)
            self.go(q, 5, across, sib)

        def end(self, q):
            other = 1 - c
            self.got(q, 2, 2 * x + other)
            self.got(q, 3, 2 * xl + other)
            self.got(q, 4, 2 * xr + other)
            self.got(q, 5, 2 * ((x + 2) % 4) + other)

        def whole(self):
            for step in (self.start, self.mid, self.far, self.end):
                for q in range(self.parts):
                    step(q)

    class Exchange:
        def __init__(self, src, dst):
            self.src, self.dst = src, dst
            self.base = sems(n_e)

        def start(self):
            for p in range(1, n_e):
                peer = 2 * ((x + p // 2) % 4) + (c + p % 2) % 2
                send(self.src(peer), self.dst(e), self.base + p, me, peer)

        def wait(self):
            for p in range(1, n_e):
                peer = 2 * ((x + 4 - p // 2) % 4) + (c + p % 2) % 2
                arrive(self.dst(peer), self.base + p)

    class Reduce:
        def __init__(self, first, n, partial, bufs):
            self.n, self.half, self.partial = n, n // 2, partial
            self.first = first
            self.sib_send, self.sib_recv, self.pair, self.xs, self.far, self.lft, self.rgt = bufs
            self.base = sems(10)

        def rows(self, ref, lead, half=None):
            if half is None:
                piece = pl.ds(pl.multiple_of(self.first, TILE), self.n)
            else:
                piece = pl.ds(pl.multiple_of(self.first + half * self.half, TILE), self.half)
            return ref.at[piece] if lead is None else ref.at[lead, piece]

        def local(self):
            for i, dx in enumerate((2, 1, 3, 0)):
                block = 2 * ((x + dx) % 4) + (1 - c)
                mine = self.rows(self.sib_send, dx)
                mine[...] = self.partial(block).astype(BF16)
                send(mine, self.rows(self.sib_recv, dx), self.base + dx, me, sib)

        def put(self, dx, half, extra, target, landing, t):
            value = self.rows(self.pair, dx, half)[...]
            if extra is not None:
                value = value + extra[...].astype(F32)
            out = self.rows(self.xs, dx, half)
            out[...] = value.astype(BF16)
            send(out, self.rows(landing, None, half), self.base + t, me, target)

        def pairs(self):
            for dx in (2, 1, 3, 0):
                block = 2 * ((x + dx) % 4) + c
                own = self.partial(block)
                theirs = self.rows(self.sib_recv, dx)
                arrive(theirs, self.base + dx)
                self.rows(self.pair, dx)[...] = own + theirs[...].astype(F32)
                if dx == 2:
                    self.put(2, 0, None, right, self.far, 4)
                    self.put(2, 1, None, left, self.far, 5)
                elif dx == 1:
                    self.put(1, 1, None, right, self.lft, 6)
                elif dx == 3:
                    self.put(3, 0, None, left, self.rgt, 7)

        def relay(self):
            arrived = self.rows(self.far, None, 0)
            arrive(arrived, self.base + 4)
            self.put(1, 0, arrived, right, self.lft, 8)
            arrived = self.rows(self.far, None, 1)
            arrive(arrived, self.base + 5)
            self.put(3, 1, arrived, left, self.rgt, 9)

        def total(self):
            arrive(self.rows(self.lft, None, 1), self.base + 6)
            arrive(self.rows(self.rgt, None, 0), self.base + 7)
            arrive(self.rows(self.lft, None, 0), self.base + 8)
            arrive(self.rows(self.rgt, None, 1), self.base + 9)
            return (
                self.rows(self.pair, 0)[...]
                + self.rows(self.lft, None)[...].astype(F32)
                + self.rows(self.rgt, None)[...].astype(F32)
            )

    local = {}

    def load(name, src, dst):
        copy_in = pltpu.make_async_copy(src, dst, ls.at[len(local)])
        copy_in.start()
        local[name] = copy_in

    load("memory", memory_hbm, mem_all.at[e])
    load("grad", grad_hbm.at[:, pl.ds(col_e, F)], live)
    load("wo", wo_hbm, wo)
    load("tokens", tokens_hbm, tok)
    load("wq", wq_hbm, wq)
    load("wk", wk_hbm, wk)
    load("wv", wv_hbm, wv)
    load("wr", wr_hbm.at[pl.ds(pl.multiple_of(e * F, F), F)], wr)
    load("down", down_hbm, down)
    load("up", up_hbm, up)

    barrier = pltpu.get_barrier_semaphore()

    def greet(kk, carry):
        pl.semaphore_signal(
            barrier, inc=1, device_id=((me + kk) % n_dp, e), device_id_type=pl.DeviceIdType.MESH
        )
        return carry

    lax.fori_loop(1, n_dp, greet, 0)
    for p in range(1, n_e):
        pl.semaphore_signal(
            barrier, inc=1, device_id=(me, (e + p) % n_e), device_id_type=pl.DeviceIdType.MESH
        )

    routing = routing_ref[...]
    choice = [routing[:, 0:1], routing[:, 1:2]]
    lane_te = iota((T, LANES), 1)
    hot = [(lane_te == choice[i]).astype(F32) for i in range(2)]
    before = (iota((T, T), 0) > iota((T, T), 1)).astype(BF16)
    counts = dot(before, (hot[0] + hot[1]).astype(BF16))
    rank = [jnp.sum(hot[i] * counts, axis=1, keepdims=True) for i in range(2)]
    slot = [choice[i].astype(F32) * CAP + rank[i] for i in range(2)]
    names = to_rows([choice[0].astype(F32), choice[1].astype(F32), rank[0], rank[1], slot[0], slot[1]])
    names = names.astype(jnp.int32)
    slot_row = iota((R, T), 0)
    plan[...] = jnp.logical_or(slot_row == names[4:5], slot_row == names[5:6]).astype(BF16)
    slot_lane = iota((T, R), 1)
    plan0[...] = (slot_lane == slot[0].astype(jnp.int32)).astype(BF16)
    plan1[...] = (slot_lane == slot[1].astype(jnp.int32)).astype(BF16)

    lane_1 = iota((1, LANES), 1)
    note = jnp.zeros((1, LANES), jnp.int32)
    for k in range(z.S):
        note = jnp.where(lane_1 == k, src_ref[k], note)
        note = jnp.where(lane_1 == z.S + k, slen_ref[k], note)
    meta[pl.ds(me, 1), :] = note.astype(F32)

    local["grad"].wait()
    row_t = iota((T, 1), 0)
    length = jnp.zeros((T, 1), jnp.int32)
    for k in range(z.S):
        length = jnp.where((row_t >> log2(z.L)) == k, tlen_ref[k], length)
    alive = (row_t & (z.L - 1)) < length
    live[...] = jnp.where(alive, live[...].astype(F32), 0.0).astype(BF16)
    slots = dot(plan[...], live[...]).astype(BF16)
    g_send[...] = slots
    own_rows = pl.ds(pl.multiple_of(me * CAP, CAP), CAP)
    g_all[e, own_rows, :] = g_send[own_rows, :]

    pl.semaphore_wait(barrier, n_dp - 1 + n_e - 1)

    def halves(ref, rows):
        return lambda b, q: ref.at[b, pl.ds(q * (rows // 2), rows // 2)]

    local["memory"].wait()
    memory_gather = Gather(halves(mem_all, T), 2)
    memory_gather.start(0)
    memory_gather.start(1)
    meta_spread = Spread(lambda t: one_row(meta, me), lambda i: one_row(meta, i))
    meta_spread.start()
    g_spread = Spread(lambda t: rows16(g_send, t), lambda i: rows16(g_all.at[e], i))
    g_spread.start()

    local["tokens"].wait()
    local["wq"].wait()
    rows_f = tok[...].astype(F32)
    centred = rows_f - jnp.mean(rows_f, axis=1, keepdims=True)
    variance = jnp.mean(centred * centred, axis=1, keepdims=True)
    normed = (centred * lax.rsqrt(variance + EPS) * again_ref[...]).astype(BF16)
    queries = dot(normed, wq[...]).astype(BF16)

    for q in range(2):
        memory_gather.mid(q)
    local["wo"].wait()
    for b in range(n_e):

        @pl.when(e == b)
        def _():
            ow_all[b] = wo[:, b * F : (b + 1) * F]

    ow_exchange = Exchange(
        lambda peer: wo.at[:, pl.ds(pl.multiple_of(peer * F, F), F)], lambda b: ow_all.at[b]
    )
    for q in range(2):
        memory_gather.far(q)
    for q in range(2):
        memory_gather.end(q)
    ow_exchange.start()

    local["wk"].wait()
    local["wv"].wait()
    keys = jnp.zeros((T, z.Hd), F32)
    values = jnp.zeros((T, z.Hd), F32)
    for b in range(n_e):
        block = mem_all[b]
        keys = keys + dot(block, wk[b * F : (b + 1) * F, :])
        values = values + dot(block, wv[b * F : (b + 1) * F, :])

    r_out = iota((2 * T, 2 * T), 0)
    r_in = iota((2 * T, 2 * T), 1)
    place = (
        ((r_out >> 3) & 1) * T + ((r_out >> 1) & 3) * z.L + ((r_out >> 4) << 1) + (r_out & 1)
    )
    order = (r_in == place).astype(BF16)

    middle_me = me % 2 == (me // 4 + c) % 2
    my_middle = me // 2

    def middle_dp(m):
        return 2 * m + (m // 2 + c) % 2

    class Relay:
        def __init__(self, send_buf, held, sorted_buf, recv_buf):
            self.send_buf, self.held, self.sorted_buf, self.recv_buf = (
                send_buf, held, sorted_buf, recv_buf,
            )
            self.out = sems(n_dp)
            self.back = sems(n_dp)

        def first(self, m):
            return copy(
                rows16(self.send_buf, m), rows16(self.held, me), self.out + me, middle_dp(m), e,
                ks=self.out + m,
            )

        def second(self, j):
            return copy(
                rows16(self.sorted_buf, j), rows16(self.recv_buf, my_middle),
                self.back + my_middle, j, e, ks=self.back + j,
            )

        def each_middle(self, action):
            def step(kk, carry):
                m = (my_middle + kk) % z.mids

                @pl.when(middle_dp(m) != me)
                def _():
                    action(m)

                return carry

            lax.fori_loop(0, z.mids, step, 0)

        def each_other(self, action):
            def step(kk, carry):
                action((me + kk) % n_dp)
                return carry

            lax.fori_loop(1, n_dp, step, 0)

        def start(self):
            self.each_middle(lambda m: self.first(m).start())

            @pl.when(middle_me)
            def _():
                rows16(self.held, me)[...] = rows16(self.send_buf, my_middle)[...]

        def turn(self, transposed):
            @pl.when(middle_me)
            def _():
                self.each_other(lambda i: arrive(rows16(self.held, i), self.out + i))
                self.sorted_buf[...] = dot(
                    relay_plan[...], self.held[...], 0 if transposed else 1, 0
                ).astype(BF16)
                self.each_other(lambda j: self.second(j).start())
                rows16(self.recv_buf, my_middle)[...] = rows16(self.sorted_buf, me)[...]

        def end(self):
            self.each_middle(lambda m: arrive(rows16(self.recv_buf, m), self.back + m))

        def finish(self):
            self.each_middle(lambda m: self.first(m).wait_send())

            @pl.when(middle_me)
            def _():
                self.each_other(lambda j: self.second(j).wait_send())

    both = jnp.concatenate([keys.astype(BF16), values.astype(BF16)], axis=0)
    kv_send[...] = dot(order, both).astype(BF16)
    relay = Relay(kv_send, mid_buf, mid_out_buf, kv_recv)
    relay.start()

    meta_spread.wait()
    notes = meta[...]
    span = n_dp * TILE
    pick = ((iota((span, n_dp), 0) >> 4) == iota((span, n_dp), 1)).astype(BF16)
    spread_notes = dot(pick, notes.astype(BF16))
    wanted = ((iota((span, LANES), 0) >> 1) & 3) == iota((span, LANES), 1)
    source = jnp.sum(jnp.where(wanted, spread_notes, 0.0), axis=1, keepdims=True).astype(jnp.int32)
    p_row = iota((span, span), 0)
    p_col = iota((span, span), 1)
    relay_plan[...] = (p_col == (source * TILE + (p_row & (TILE - 1)))).astype(BF16)
    relay.turn(False)

    g_spread.wait()
    g_gather = Gather(halves(g_all, R), 2)
    g_gather.start(0)
    g_gather.start(1)

    key_length = jnp.zeros((1, T), F32)
    key_at = iota((1, T), 1)
    n_row, n_lane = iota((n_dp, LANES), 0), iota((n_dp, LANES), 1)
    for k in range(z.S):
        here = jnp.logical_and(n_row == src_ref[k], n_lane == z.S + k)
        found = jnp.sum(jnp.where(here, notes, 0.0), axis=1, keepdims=True)
        found = jnp.sum(found, axis=0, keepdims=True)
        key_length = jnp.where((key_at >> log2(z.L)) == k, found, key_length)

    relay.end()
    kv = dot(order, kv_recv[...], 0, 0).astype(BF16)
    key_heads, value_heads = kv[:T], kv[T:]

    scaling = z.Hd ** (-0.5)
    same = (iota((T, T), 0) >> log2(z.L)) == (iota((T, T), 1) >> log2(z.L))
    inside = (key_at & (z.L - 1)).astype(F32) < key_length
    open_keys = jnp.logical_and(same, inside)
    scores = jnp.where(open_keys, dot(queries, key_heads, 1, 1) * scaling, -1e30)
    exps = jnp.exp(scores - jnp.max(scores, axis=1, keepdims=True))
    probabilities = exps / jnp.sum(exps, axis=1, keepdims=True)
    weights = probabilities.astype(BF16)
    att_all[e] = dot(weights, value_heads).astype(BF16)
    att_gather = Gather(halves(att_all, T), 2)
    for q in range(2):
        att_gather.start(q)
    for q in range(2):
        att_gather.mid(q)
    for q in range(2):
        att_gather.far(q)
    for q in range(2):
        g_gather.mid(q)
    ow_exchange.wait()
    for q in range(2):
        att_gather.end(q)

    heads_sum = jnp.zeros((T, F), F32)
    for b in range(n_e):
        heads_sum = heads_sum + dot(att_all[b], ow_all[b])
    hidden = (tok[:, pl.ds(col_e, F)].astype(F32) + heads_sum).astype(BF16).astype(F32)
    hid[...] = hidden
    part_sum = jnp.sum(hidden, axis=1, keepdims=True)
    off = hidden - part_sum * (1.0 / F)
    part_sq = jnp.sum(off * off, axis=1, keepdims=True)
    stat1[e] = to_rows([part_sum, part_sq])
    stat1_exchange = Exchange(lambda peer: stat1.at[e], lambda b: stat1.at[b])
    stat1_exchange.start()
    for q in range(2):
        g_gather.far(q)
    for q in range(2):
        g_gather.end(q)
    stat1_exchange.wait()
    parts = [stat1[b] for b in range(n_e)]
    mean_row = sum(p[0:1] for p in parts) * (1.0 / D)
    square_row = sum(p[1:2] for p in parts)
    for p in parts:
        shift = p[0:1] * (1.0 / F) - mean_row
        square_row = square_row + F * (shift * shift)
    rstd_row = lax.rsqrt(square_row * (1.0 / D) + EPS)
    mean, rstd = to_columns(stack_rows(mean_row, rstd_row), 2)
    gain = fgain_ref[:, pl.ds(col_e, F)]
    unit = (hidden - mean) * rstd
    expert_in = (unit * gain).astype(BF16)

    x_send[...] = dot(plan[...], expert_in).astype(BF16)
    x_all[e, own_rows, :] = x_send[own_rows, :]
    x_spread = Spread(lambda t: rows16(x_send, t), lambda i: rows16(x_all.at[e], i))
    x_spread.start()
    local["wr"].wait()
    router = wr[...]
    logit_part = dot(expert_in, router)
    wide = jnp.concatenate([logit_part, jnp.zeros((T, LANES - z.E), F32)], axis=1)
    lg_all[e] = wide.T[: z.E]
    lg_exchange = Exchange(lambda peer: lg_all.at[e], lambda b: lg_all.at[b])
    lg_exchange.start()

    local["down"].wait()

    def down_back(q, carry):
        piece = pl.ds(pl.multiple_of(q * Q, Q), Q)
        total = jnp.zeros((Q, z.H), F32)
        for b in range(n_e):
            total = total + dot(g_all[b, piece, :], down[:, b * F : (b + 1) * F], 1, 1)
        u_buf[piece, :] = total
        return carry

    lax.fori_loop(0, 2, down_back, 0)

    lg_exchange.wait()
    logits = sum(lg_all[b] for b in range(n_e))
    expert_row = iota((z.E, T), 0)
    hot_rows = [expert_row == names[i : i + 1] for i in range(2)]
    chosen = [jnp.sum(jnp.where(h, logits, 0.0), axis=0, keepdims=True) for h in hot_rows]
    top = jnp.maximum(chosen[0], chosen[1])
    lifted = [jnp.exp(v - top) for v in chosen]
    share = [v / (lifted[0] + lifted[1]) for v in lifted]
    rank_lane = [
        (iota((T, LANES), 1) == rank[i].astype(jnp.int32)).astype(F32) for i in range(2)
    ]
    gate_rows = jnp.zeros((z.E, LANES), F32)
    for i in range(2):
        gate_rows = gate_rows + dot(jnp.where(hot_rows[i], share[i], 0.0), rank_lane[i], 1, 0, HI)
    gate_send[...] = gate_rows
    gate_recv[pl.ds(me, 1), :] = gate_send[pl.ds(me, 1), :]
    gate_spread = Spread(lambda t: one_row(gate_send, t), lambda i: one_row(gate_recv, i))
    gate_spread.start()
    lax.fori_loop(2, GROUPS, down_back, 0)

    def group_first(k):
        return ((my_group + GROUPS - k) % GROUPS) * Q

    x_gather = Gather(lambda b, k: x_all.at[b, pl.ds(pl.multiple_of(group_first(k), Q), Q)], GROUPS)
    local["up"].wait()
    reduces = []

    def expert_group(k):
        first = group_first(k)
        piece = pl.ds(pl.multiple_of(first, Q), Q)
        pre = jnp.zeros((Q, z.H), F32)
        for b in range(n_e):
            pre = pre + dot(x_all[b, piece, :], up[b * F : (b + 1) * F, :])
        cubic = pre * pre * pre
        slope_in = 0.7978845608028654 * (pre + 0.044715 * cubic)
        bend = jnp.tanh(slope_in)
        act = (pre * (0.5 * (1.0 + bend))).astype(BF16)
        act_buf[piece, :] = act
        slope = 0.5 * (1.0 + bend) + 0.5 * pre * (1.0 - bend * bend) * (
            0.7978845608028654 * (1.0 + 3.0 * 0.044715 * pre * pre)
        )
        grads = u_buf[piece, :]
        gates, pick, wanted = gate_column(first, Q)
        pg_buf[piece, :] = (gates * grads * slope).astype(BF16)
        dots = jnp.sum(act.astype(F32) * grads, axis=1, keepdims=True)
        return dot(pick, jnp.where(wanted, dots, 0.0), 0, 0, HI)

    def gate_column(first, rows):
        pick = (((iota((rows, n_dp), 0) + first) >> 4) == iota((rows, n_dp), 1)).astype(F32)
        wanted = (iota((rows, LANES), 0) & (CAP - 1)) == iota((rows, LANES), 1)
        spread_gates = dot(pick, gate_recv[...], 1, 0, HI)
        gates = jnp.sum(jnp.where(wanted, spread_gates, 0.0), axis=1, keepdims=True)
        return gates, pick, wanted

    def input_partial(first):
        def partial(block):
            piece = pl.ds(pl.multiple_of(first, Q), Q)
            rows = pl.ds(pl.multiple_of(block * F, F), F)
            return dot(pg_buf[piece, :], up[rows, :], 1, 1)

        return partial

    ret_spread = Spread(lambda t: rows16(ret_send, t), lambda i: rows16(ret_recv, i))
    ret_spread.finish_later()
    bufs = (sib_send, sib_recv, pair, xs_send, far_recv, lft_recv, rgt_recv)

    def give_back(k):
        first = group_first(k)
        piece = pl.ds(pl.multiple_of(first, Q), Q)
        ret_send[piece, :] = reduces[k].total().astype(BF16)
        ret_spread.start_group((my_group + GROUPS - k) % GROUPS)

    gg_total = jnp.zeros((n_dp, LANES), F32)
    for step in range(GROUPS + 3):
        if step < GROUPS:
            x_spread.wait_group((my_group + GROUPS - step) % GROUPS)
            x_gather.start(step)
        if 1 <= step < GROUPS + 1:
            x_gather.mid(step - 1)
        if 2 <= step < GROUPS + 2:
            x_gather.far(step - 2)
        if step == 2:
            gate_spread.wait()
        if step >= 3:
            k = step - 3
            x_gather.end(k)
            gg_total = gg_total + expert_group(k)
            reduces.append(Reduce(group_first(k), Q, input_partial(group_first(k)), bufs))
            reduces[k].local()
            reduces[k].pairs()
            if k >= 1:
                reduces[k - 1].relay()

    gg_all[e] = gg_total
    gg_exchange = Exchange(lambda peer: gg_all.at[e], lambda b: gg_all.at[b])
    gg_exchange.start()
    reduces[GROUPS - 1].relay()

    def up_back(b, carry):
        rows = pl.ds(pl.multiple_of(b * F, F), F)
        ug[rows, :] = dot(x_all[b], pg_buf[...], 0, 0).astype(BF16)
        return carry

    gates_all = gate_column(0, R)[0]

    def down_grad(b, carry):
        columns = pl.ds(pl.multiple_of(b * F, F), F)
        scaled = (g_all[b].astype(F32) * gates_all).astype(BF16)
        dg[:, columns] = dot(act_buf[...], scaled, 0, 0).astype(BF16)
        return carry

    give_back(0)
    gg_exchange.wait()
    gg_sum = sum(gg_all[b] for b in range(n_e))
    gg_send[...] = gg_sum
    gg_recv[pl.ds(me, 1), :] = gg_send[pl.ds(me, 1), :]
    gg_spread = Spread(lambda t: one_row(gg_send, t), lambda i: one_row(gg_recv, i))
    gg_spread.start()
    give_back(1)
    lax.fori_loop(0, n_e // 2, up_back, 0)
    give_back(2)
    lax.fori_loop(n_e // 2, n_e, up_back, 0)
    give_back(3)
    ret_recv[own_rows, :] = ret_send[own_rows, :]
    up_store = pltpu.make_async_copy(ug, up_out, ls.at[len(local)])
    up_store.start()
    lax.fori_loop(0, n_e // 2, down_grad, 0)

    gg_spread.wait()
    gate_grad = []
    for i in range(2):
        spread_gg = dot(gg_recv[...], rank_lane[i], 1, 1, HI)
        gate_grad.append(jnp.sum(jnp.where(hot_rows[i], spread_gg, 0.0), axis=0, keepdims=True))
    delta = share[0] * share[1] * (gate_grad[0] - gate_grad[1])
    logit_grad = jnp.where(hot_rows[0], delta, 0.0) - jnp.where(hot_rows[1], delta, 0.0)
    high = logit_grad.astype(BF16)
    low = (logit_grad - high.astype(F32)).astype(BF16)
    router_term = dot(high, router, 0, 1) + dot(low, router, 0, 1)
    share_columns = to_columns(stack_rows(share[0], share[1]), 2)

    ret_spread.wait()
    returned = ret_recv[...]
    ffn_in_grad = (
        share_columns[0] * dot(plan0[...], returned)
        + share_columns[1] * dot(plan1[...], returned)
        + router_term
    )

    scaled_in = ffn_in_grad * gain
    unit = (hid[...] - mean) * rstd
    stat2[e] = to_rows(
        [
            jnp.sum(scaled_in, axis=1, keepdims=True),
            jnp.sum(scaled_in * unit, axis=1, keepdims=True),
        ]
    )
    stat2_exchange = Exchange(lambda peer: stat2.at[e], lambda b: stat2.at[b])
    stat2_exchange.start()
    lax.fori_loop(n_e // 2, n_e, down_grad, 0)
    down_store = pltpu.make_async_copy(dg, down_out, ls.at[len(local) + 1])
    down_store.start()
    stat2_exchange.wait()
    sums = sum(stat2[b] for b in range(n_e)) * (1.0 / D)
    mean_in, mean_unit = to_columns(sums, 2)
    hidden_grad = live[...].astype(F32) + rstd * (scaled_in - mean_in - unit * mean_unit)
    hg_all[e] = hidden_grad.astype(BF16)
    hg_gather = Gather(halves(hg_all, T), 2)
    hg_gather.whole()

    att_grad = jnp.zeros((T, z.Hd), F32)
    for b in range(n_e):
        att_grad = att_grad + dot(hg_all[b], wo[:, b * F : (b + 1) * F], 1, 1)
    att_grad = att_grad.astype(BF16)
    value_grad = dot(weights, att_grad, 0, 0).astype(BF16)
    prob_grad = dot(att_grad, value_heads, 1, 1)
    inner = jnp.sum(probabilities * prob_grad, axis=1, keepdims=True)
    score_grad = (probabilities * (prob_grad - inner) * scaling).astype(BF16)
    key_grad = dot(score_grad, queries, 0, 0).astype(BF16)
    both = jnp.concatenate([key_grad, value_grad], axis=0)
    kvg_send[...] = dot(order, both).astype(BF16)
    relay_back = Relay(kvg_send, mid_buf2, mid_out2, kvg_recv)
    relay_back.start()
    relay_back.turn(True)
    relay_back.end()
    home = dot(order, kvg_recv[...], 0, 0).astype(BF16)
    home_keys, home_values = home[:T], home[T:]

    def memory_partial(block):
        rows = pl.ds(pl.multiple_of(block * F, F), F)
        return dot(home_keys, wk[rows, :], 1, 1) + dot(home_values, wv[rows, :], 1, 1)

    memory_reduce = Reduce(
        0, T, memory_partial,
        (m_sib_send, m_sib_recv, m_pair, m_xs_send, m_far_recv, m_lft_recv, m_rgt_recv),
    )
    memory_reduce.local()
    memory_reduce.pairs()
    memory_reduce.relay()
    mg[...] = memory_reduce.total().astype(BF16)
    mem_store = pltpu.make_async_copy(mg, mem_out, ls.at[len(local) + 2])
    mem_store.start()

    relay.finish()
    relay_back.finish()
    for finish in pending:
        finish()
    up_store.wait()
    down_store.wait()
    mem_store.wait()
    assert counter[0] <= SEMS, counter[0]


SEMS = 512


def build(mesh):
    n_dp, n_e = mesh.shape["dp"], mesh.shape["expert"]

    def body(
        tokens, memory, source_length, owner_device, source_device, target_length, routing,
        attn_gain, ffn_gain, query_weight, key_weight, value_weight, out_weight, router_weight,
        up_weight, down_weight, grad_out,
    ):
        sentences, length, width = tokens.shape
        z = Layout(
            n_dp, n_e, sentences, length, width, query_weight.shape[1], up_weight.shape[2],
            router_weight.shape[1],
        )
        T, D, F, R, H = z.T, z.D, z.F, z.R, z.H
        span = n_dp * TILE
        vm = pltpu.VMEM
        scratch = [
            vm((T, D), BF16), vm((T, F), BF16), vm((D, z.Hd), BF16), vm((D, z.Hd), BF16),
            vm((D, z.Hd), BF16), vm((z.Hd, D), BF16), vm((F, z.E), BF16), vm((D, H), BF16),
            vm((H, D), BF16),
            vm((n_e, T, F), BF16), vm((n_e, z.Hd, F), BF16), vm((n_e, T, z.Hd), BF16),
            vm((n_e, T, F), BF16), vm((n_e, R, F), BF16), vm((n_e, R, F), BF16),
            vm((R, F), BF16), vm((R, F), BF16), vm((R, F), BF16), vm((R, F), BF16),
            vm((n_dp, LANES), F32),
            vm((2 * T, z.Hd), BF16), vm((span, z.Hd), BF16), vm((span, z.Hd), BF16),
            vm((2 * T, z.Hd), BF16),
            vm((2 * T, z.Hd), BF16), vm((span, z.Hd), BF16), vm((span, z.Hd), BF16),
            vm((2 * T, z.Hd), BF16),
            vm((n_e, 8, T), F32), vm((n_e, 8, T), F32), vm((n_e, z.E, T), F32),
            vm((z.E, LANES), F32), vm((n_dp, LANES), F32), vm((n_e, n_dp, LANES), F32),
            vm((n_dp, LANES), F32), vm((n_dp, LANES), F32),
            vm((R, T), BF16), vm((T, R), BF16), vm((T, R), BF16), vm((span, span), BF16),
            vm((R, H), F32), vm((R, H), BF16), vm((R, H), BF16),
            vm((4, R, F), BF16), vm((4, R, F), BF16), vm((4, R, F), F32), vm((4, R, F), BF16),
            vm((R, F), BF16), vm((R, F), BF16), vm((R, F), BF16),
            vm((4, T, F), BF16), vm((4, T, F), BF16), vm((4, T, F), F32), vm((4, T, F), BF16),
            vm((T, F), BF16), vm((T, F), BF16), vm((T, F), BF16),
            vm((D, H), BF16), vm((H, D), BF16), vm((T, F), BF16), vm((T, F), F32),
            pltpu.SemaphoreType.DMA((SEMS,)), pltpu.SemaphoreType.DMA((SEMS,)),
            pltpu.SemaphoreType.DMA((16,)),
        ]
        smem = pl.BlockSpec(memory_space=pltpu.SMEM)
        vmem = pl.BlockSpec(memory_space=pltpu.VMEM)
        hbm = pl.BlockSpec(memory_space=pl.ANY)
        mem_grad, up_grad, down_grad = pl.pallas_call(
            functools.partial(layer_kernel, z),
            out_shape=(
                jax.ShapeDtypeStruct((T, F), BF16),
                jax.ShapeDtypeStruct((D, H), BF16),
                jax.ShapeDtypeStruct((H, D), BF16),
            ),
            in_specs=[smem] * 3 + [vmem] * 3 + [hbm] * 10,
            out_specs=(hbm, hbm, hbm),
            scratch_shapes=scratch,
            compiler_params=pltpu.CompilerParams(
                collective_id=0, has_side_effects=True, vmem_limit_bytes=56 * 1024 * 1024
            ),
            name="layer",
        )(
            source_device, source_length, target_length, routing.reshape(T, 2),
            attn_gain[None], ffn_gain[None],
            tokens.reshape(T, D), memory.reshape(T, F), grad_out.reshape(T, D),
            query_weight, key_weight, value_weight, out_weight, router_weight,
            up_weight[0], down_weight[0],
        )
        return mem_grad.reshape(sentences, length, F), up_grad[None], down_grad[None]

    return body


def solution(mesh):
    in_specs = (
        P("dp", None, None),
        P("dp", None, "expert"),
        P("dp"),
        P("dp"),
        P("dp"),
        P("dp"),
        P("dp", None, None),
        P(),
        P(),
        P(None, "expert"),
        P(None, "expert"),
        P(None, "expert"),
        P("expert", None),
        P(),
        P("dp", None, "expert"),
        P("dp", "expert", None),
        P("dp", None, None),
    )
    out_specs = (P("dp", None, "expert"), P("dp", None, "expert"), P("dp", "expert", None))
    return jax.shard_map(
        build(mesh), mesh=mesh, in_specs=in_specs, out_specs=out_specs, check_vma=False
    )
```

time: 605 us -> 151 us (0.25)
  blocking collectives: 239 us -> 0 us
  waiting for transfers between devices: 232 us -> 0 us
  Pallas kernels: 0 us -> 139 us
  matrix products: 34 us -> 0 us
  starting transfers between devices: 31.3 us -> 0 us
  local copies, waits for them, and re-layouts: 33.2 us -> 9.31 us
  other arithmetic: 14.9 us -> 0 us
  between operations: 14.9 us -> 0.64 us
    all_to_all x4 -> x0, blocking collectives: 222 us -> none  [the longest x2 115 us: send_slots(): lax.all_to_all(builder(0, capacity), 'dp', split_axis=0, concat_axis=0, t...]
    pallas_call x0 -> x1, Pallas kernels: none -> 139 us  [body(): pl.pallas_call(functools.partial(layer_kernel, z), out_shape=(jax.ShapeDt...]
    reduce_scatter x3 -> x0, waiting for transfers between devices: 101 us -> none  [the longest x2 69.6 us: reduce_slices(): lax.psum_scatter(widened.astype(jnp.bfloat16), 'expert', scatter_dimensio...]
    psum x1 -> x0, waiting for transfers between devices: 58.6 us -> none  [body(): lax.psum(partial_value.astype(jnp.bfloat16), 'expert').astype(jnp.float32)]
    all_gather x2 -> x0, waiting for transfers between devices: 53.4 us -> none  [sum_slices(): filled = lax.all_gather(summed, 'expert', axis=1, tiled=True)]
    dot_general x31 -> x0, matrix products: 33.2 us -> none  [the longest x1 4.35 us: body(): jnp.einsum('rd,rf->df', slots_in, pre_grad, preferred_element_type=jnp.fl...]
    all_to_all x3 -> x0, starting transfers between devices: 30.8 us -> none  [the longest x1 12 us: body(): lax.all_to_all(outbound_len, 'dp', split_axis=0, concat_axis=0, tiled=True)]
    all_to_all x3 -> x0, waiting for transfers between devices: 19.1 us -> none  [the longest x1 13 us: body(): lax.all_to_all(outbound, 'dp', split_axis=0, concat_axis=0, tiled=True)]
  transfers between devices with their start and end apart: 9 -> 0, of which waited for: 8 -> 0; matrix products, arithmetic and copies ran while one was open for 5% -> 0% of each run, Pallas kernels for 0% -> 0%
where the time goes in v1:
time: 151 us; the launch traced here: 149 us
  Pallas kernels  139 us (92%)
  local copies, waits for them, and re-layouts  9.31 us (6%)
    pallas_call x1, Pallas kernels, body(): pl.pallas_call(functools.partial(layer_kernel, z), out_shape=(jax.ShapeDt...  139 us
    unnamed x7, local copies, waits for them, and re-layouts  9.31 us

profile of v1, /device:TPU:1, one launch (start us, length us, event | category | flops | bytes accessed | tf_op | source)
XLA Modules:
  0.0 149.1 jit_solution(15197005498058961555)
XLA Ops:
  0.6 1.4 copy.19
  2.0 1.9 %copy.20.wr_hbm = bf16[2048,32]{1,0:T(8,128)(2,1)} copy(bf16[2048,32]{0,1:T(8,128)(2,1)} %param.29) | data formatting | bytes 262144 | tf_op args[13]
  4.0 139.1 %layer.1 = (bf16[128,256]{1,0:T(8,128)(2,1)}, bf16[2048,512]{1,0:T(8,128)(2,1)}, bf16[512,2048]{1,0:T(8,128)(2,1)}) custom-call(s32[4]{0:T(128)} %src_ref.1, s32[4]{0:T(128)} %slen_ref.1, s32[4]{0:T(128)} %tlen_ref.1, s32[128,2]{1,0:T(8,128)} %bitcast.17, f32[1,2048]{1,0:T(1,128)} %bitcast.20, f32[1,2048]{1,0:T(1,128)} %bitcast.21, ...), custom_call_target="tpu_custom_call" | custom-call | tf_op jit(solution)/shard_map/layer/pallas_call | solution.py:876
  143.1 1.5 copy.24
  144.6 0.0 copy-start
  144.6 3.2 %copy.25 = bf16[1,2048,512]{2,1,0:T(8,128)(2,1)} copy(bf16[1,2048,512]{2,1,0:T(8,128)(2,1)} %bitcast.12) | data formatting | bytes 4194304
  147.8 0.0 copy-done
  147.8 1.3 copy.26
Async XLA Ops:
  144.6 3.2 %copy-start = (bf16[512,2048]{1,0:T(8,128)(2,1)S(1)}, bf16[512,2048]{1,0:T(8,128)(2,1)}, u32[]{:S(2)}) copy-start(bf16[512,2048]{1,0:T(8,128)(2,1)} %get-tuple-element.8) | copy-start | bytes 6291460

commit v2 on v1

v2 whole, which is shorter than its diff:
```python
import functools

import jax
import jax.numpy as jnp
from jax import lax
from jax.experimental import pallas as pl
from jax.experimental.pallas import tpu as pltpu
from jax.sharding import PartitionSpec as P

F32 = jnp.float32
BF16 = jnp.bfloat16
HI = lax.Precision.HIGHEST
LANES = 128
CAP = 16
TILE = 16
GROUPS = 4
EPS = 1e-5


def dot(a, b, ca=1, cb=0, precision=None):
    return lax.dot_general(
        a, b, (((ca,), (cb,)), ((), ())), preferred_element_type=F32, precision=precision
    )


def iota(shape, dim):
    return lax.broadcasted_iota(jnp.int32, shape, dim)


def log2(value):
    return value.bit_length() - 1


def to_rows(columns):
    rows = columns[0].shape[0]
    lane = iota((rows, LANES), 1)
    packed = jnp.zeros((rows, LANES), F32)
    for i, column in enumerate(columns):
        packed = jnp.where(lane == i, column, packed)
    return packed.T[:8]


def to_columns(rows, count):
    padded = jnp.concatenate([rows, jnp.zeros((LANES - 8, rows.shape[1]), F32)], axis=0).T
    return [padded[:, i : i + 1] for i in range(count)]


def stack_rows(*rows):
    fill = jnp.zeros((8 - len(rows), rows[0].shape[1]), F32)
    return jnp.concatenate([*rows, fill], axis=0)


class Layout:
    def __init__(self, n_dp, n_e, sentences, length, width, head, hidden, experts):
        self.n_dp, self.n_e, self.n_x = n_dp, n_e, n_e // 2
        self.S, self.L, self.T = sentences, length, sentences * length
        self.D, self.F = width, width // n_e
        self.Hd, self.H, self.E = head, hidden, experts
        self.R = n_dp * CAP
        self.mids = n_dp // 2
        self.gs = n_dp // GROUPS
        self.Q = self.R // GROUPS


def layer_kernel(
    z,
    src_ref, slen_ref, tlen_ref, routing_ref, again_ref, fgain_ref,
    tokens_hbm, memory_hbm, grad_hbm, wq_hbm, wk_hbm, wv_hbm, wo_hbm, wr_hbm, up_hbm, down_hbm,
    mem_out, up_out, down_out,
    tok, live, wq, wk, wv, wo, wr, up, down,
    mem_all, ow_all, att_all, hg_all, x_all, g_all,
    g_send, x_send, ret_send, ret_recv,
    meta, kv_send, mid_buf, mid_out_buf, kv_recv, kvg_send, mid_buf2, mid_out2, kvg_recv,
    stat1, stat2, lg_all, gate_send, gate_recv, gg_all, gg_send, gg_recv,
    plan, plan0, plan1, relay_plan, u_buf, act_buf, pg_buf,
    sib_send, sib_recv, own_sum, xs_send, xs_recv, uw_send, uw_recv, mg_send, mg_recv,
    ug, dg, mg, hid,
    ss, rs, ls,
):
    n_dp, n_e, T, D, F, R, Q = z.n_dp, z.n_e, z.T, z.D, z.F, z.R, z.Q
    me = lax.axis_index("dp")
    e = lax.axis_index("expert")
    x, c = e // 2, e % 2
    xr, xl = (x + 1) % 4, (x + 3) % 4
    sib = 2 * x + (1 - c)
    right, left = 2 * xr + c, 2 * xl + c
    across = 2 * ((x + 2) % 4) + c
    my_group = me // z.gs
    col_e = pl.multiple_of(e * F, F)

    counter = [0, 0]

    def sems(count):
        first = counter[0]
        counter[0] += count
        return first

    def send_sem():
        counter[1] += 1
        return counter[1] - 1

    def copy(src, dst, ks, k, dp, ex):
        return pltpu.make_async_remote_copy(
            src_ref=src,
            dst_ref=dst,
            send_sem=ss.at[ks],
            recv_sem=rs.at[k],
            device_id=(dp, ex),
            device_id_type=pl.DeviceIdType.MESH,
        )

    pending = []

    def sent(ref, ks):
        copy(ref, ref, ks, 0, me, sib).wait_send()

    def sent_later(ref, ks):
        pending.append(lambda: sent(ref, ks))

    def arrive(dst, k):
        copy(dst, dst, 0, k, me, sib).wait_recv()

    def rows16(ref, i):
        return ref.at[pl.ds(pl.multiple_of(i * CAP, CAP), CAP)]

    def one_row(ref, i):
        return ref.at[pl.ds(i, 1)]

    def some16(ref):
        return lambda i, count: ref.at[pl.ds(pl.multiple_of(i * CAP, CAP), count * CAP)]

    def some_rows(ref):
        return lambda i, count: ref.at[pl.ds(i, count)]

    class Spread:
        def __init__(self, src, dst, some, by_group=False):
            self.src, self.dst, self.some, self.by_group = src, dst, some, by_group
            self.ks = send_sem()
            self.base = sems(GROUPS if by_group else 1)
            sent_later(some(0, n_dp - 1), self.ks)

        def start_group(self, group, k):
            arrival = self.base + (my_group if self.by_group else 0)

            def step(kk, carry):
                t = group * z.gs + (me % z.gs + kk) % z.gs
                copy(self.src(t), self.dst(me), self.ks, arrival, t, e).start()
                return carry

            lax.fori_loop(1 if k == 0 else 0, z.gs, step, 0)

        def start(self):
            for k in range(GROUPS):
                self.start_group((my_group + k) % GROUPS, k)

        def wait_group(self, group, k):
            count = z.gs - 1 if k == 0 else z.gs
            if count:
                arrive(self.some(group * z.gs, count), self.base + group)

        def wait(self):
            arrive(self.some(0, n_dp - 1), self.base)

    class Gather:
        def __init__(self, ref, first, rows):
            self.ref, self.first, self.rows = ref, first, rows
            self.parts = ref.shape[1] // rows
            self.ks = send_sem()
            self.base = sems(4 * self.parts)
            sent_later(ref.at[pl.ds(0, 7)], self.ks)

        def part(self, block, q):
            return self.ref.at[block, pl.ds(pl.multiple_of(self.first(q), TILE), self.rows)]

        def go(self, q, t, block, peer):
            ref = self.part(block, q)
            copy(ref, ref, self.ks, self.base + 4 * q + t, me, peer).start()

        def start(self, q):
            self.go(q, 2, e, across)
            self.go(q, 0, e, right)
            self.go(q, 1, e, left)
            self.go(q, 3, e, sib)

        def mid(self, q):
            for t, block in ((0, left), (1, right), (2, across)):
                arrive(self.part(block, q), self.base + 4 * q + t)
                self.go(q, 3, block, sib)

        def end(self, q):
            four = self.ref.at[pl.ds(0, 4), pl.ds(pl.multiple_of(self.first(q), TILE), self.rows)]
            arrive(four, self.base + 4 * q + 3)

        def whole(self):
            for step in (self.start, self.mid, self.end):
                for q in range(self.parts):
                    step(q)

    class Exchange:
        def __init__(self, src, dst, ref):
            self.src, self.dst, self.ref = src, dst, ref
            self.ks = send_sem()
            self.base = sems(1)
            sent_later(ref.at[pl.ds(0, n_e - 1)], self.ks)

        def start(self, prepare=None):
            for p in (4, 5, 2, 3, 6, 7, 1):
                peer = 2 * ((x + p // 2) % 4) + (c + p % 2) % 2
                if prepare is not None:
                    prepare(peer)
                copy(self.src(peer), self.dst(e), self.ks, self.base, me, peer).start()

        def wait(self):
            arrive(self.ref.at[pl.ds(0, n_e - 1)], self.base)

    class Reduce:
        def __init__(self, first, n, partial, bufs):
            self.n, self.partial, self.first = n, partial, first
            self.sib_send, self.sib_recv, self.own, self.xs, self.landing = bufs
            self.ks = send_sem()
            self.base = sems(5)
            sent_later(x_all.at[pl.ds(0, 7), pl.ds(0, n)], self.ks)

        def piece(self):
            return pl.ds(pl.multiple_of(self.first, TILE), self.n)

        def local(self):
            for dx in (2, 1, 3, 0):
                block = 2 * ((x + dx) % 4) + (1 - c)
                mine = self.sib_send.at[dx, self.piece()]
                mine[...] = self.partial(block).astype(BF16)
                theirs = self.sib_recv.at[dx, self.piece()]
                copy(mine, theirs, self.ks, self.base + dx, me, sib).start()

        def pairs(self):
            for dx in (2, 1, 3, 0):
                there = 2 * ((x + dx) % 4) + c
                own = self.partial(there)
                theirs = self.sib_recv.at[dx, self.piece()]
                arrive(theirs, self.base + dx)
                both = own + theirs[...].astype(F32)
                if dx == 0:
                    self.own[self.piece(), :] = both
                else:
                    out = self.xs.at[dx - 1, self.piece()]
                    out[...] = both.astype(BF16)
                    to = self.landing.at[dx - 1, self.piece()]
                    copy(out, to, self.ks, self.base + 4, me, there).start()

        def total(self):
            arrive(self.landing.at[pl.ds(0, 3), self.piece()], self.base + 4)
            value = self.own[self.piece(), :]
            for i in range(3):
                value = value + self.landing[i, self.piece(), :].astype(F32)
            return value

    local = {}

    def load(name, src, dst):
        copy_in = pltpu.make_async_copy(src, dst, ls.at[len(local)])
        copy_in.start()
        local[name] = copy_in

    load("memory", memory_hbm, mem_all.at[e])
    load("grad", grad_hbm.at[:, pl.ds(col_e, F)], live)
    load("wo", wo_hbm, wo)
    load("tokens", tokens_hbm, tok)
    load("wq", wq_hbm, wq)
    load("wk", wk_hbm, wk)
    load("wv", wv_hbm, wv)
    load("wr", wr_hbm.at[:, pl.ds(col_e, F)], wr)
    load("down", down_hbm, down)
    load("up", up_hbm, up)

    barrier = pltpu.get_barrier_semaphore()

    def greet(kk, carry):
        pl.semaphore_signal(
            barrier, inc=1, device_id=((me + kk) % n_dp, e), device_id_type=pl.DeviceIdType.MESH
        )
        return carry

    lax.fori_loop(1, n_dp, greet, 0)
    for p in range(1, n_e):
        pl.semaphore_signal(
            barrier, inc=1, device_id=(me, (e + p) % n_e), device_id_type=pl.DeviceIdType.MESH
        )

    choice_rows = jnp.concatenate([routing_ref[s] for s in range(z.S)], axis=1)
    expert_row = iota((z.E, T), 0)
    hot_rows = [expert_row == choice_rows[i : i + 1] for i in range(2)]
    hot = [h.astype(F32) for h in hot_rows]
    before = (iota((T, T), 0) < iota((T, T), 1)).astype(BF16)
    counts = dot((hot[0] + hot[1]).astype(BF16), before)
    rank_rows = [jnp.sum(h * counts, axis=0, keepdims=True) for h in hot]
    slot_rows = [choice_rows[i : i + 1].astype(F32) * CAP + rank_rows[i] for i in range(2)]
    rank0, rank1, slot0, slot1 = to_columns(stack_rows(*rank_rows, *slot_rows), 4)
    rank, slot = [rank0, rank1], [slot0, slot1]
    slot_row = iota((R, T), 0)
    plan[...] = jnp.logical_or(slot_row == slot_rows[0].astype(jnp.int32), slot_row == slot_rows[1].astype(jnp.int32)).astype(BF16)
    slot_lane = iota((T, R), 1)
    plan0[...] = (slot_lane == slot[0].astype(jnp.int32)).astype(BF16)
    plan1[...] = (slot_lane == slot[1].astype(jnp.int32)).astype(BF16)

    lane_1 = iota((1, LANES), 1)
    note = jnp.zeros((1, LANES), jnp.int32)
    for k in range(z.S):
        note = jnp.where(lane_1 == k, src_ref[k], note)
        note = jnp.where(lane_1 == z.S + k, slen_ref[k], note)
    meta[pl.ds(me, 1), :] = note.astype(F32)

    local["grad"].wait()
    row_t = iota((T, 1), 0)
    length = jnp.zeros((T, 1), jnp.int32)
    for k in range(z.S):
        length = jnp.where((row_t >> log2(z.L)) == k, tlen_ref[k], length)
    alive = (row_t & (z.L - 1)) < length
    live[...] = jnp.where(alive, live[...].astype(F32), 0.0).astype(BF16)
    slots = dot(plan[...], live[...]).astype(BF16)
    g_send[...] = slots
    own_rows = pl.ds(pl.multiple_of(me * CAP, CAP), CAP)
    g_all[e, own_rows, :] = g_send[own_rows, :]

    pl.semaphore_wait(barrier, n_dp - 1 + n_e - 1)

    local["memory"].wait()
    memory_gather = Gather(mem_all, lambda q: q * (T // 2), T // 2)
    memory_gather.start(0)
    memory_gather.start(1)
    meta_spread = Spread(lambda t: one_row(meta, me), lambda i: one_row(meta, i), some_rows(meta))
    meta_spread.start()
    g_spread = Spread(
        lambda t: rows16(g_send, t), lambda i: rows16(g_all.at[e], i), some16(g_all.at[e])
    )
    g_spread.start()

    local["tokens"].wait()
    local["wq"].wait()
    rows_f = tok[...].astype(F32)
    centred = rows_f - jnp.mean(rows_f, axis=1, keepdims=True)
    variance = jnp.mean(centred * centred, axis=1, keepdims=True)
    normed = (centred * lax.rsqrt(variance + EPS) * again_ref[...]).astype(BF16)
    queries = dot(normed, wq[...]).astype(BF16)

    local["wo"].wait()
    for b in range(n_e):

        @pl.when(e == b)
        def _():
            ow_all[b] = wo[:, b * F : (b + 1) * F]

    ow_exchange = Exchange(
        lambda peer: wo.at[:, pl.ds(pl.multiple_of(peer * F, F), F)],
        lambda b: ow_all.at[b],
        ow_all,
    )
    for q in range(2):
        memory_gather.mid(q)
    for q in range(2):
        memory_gather.end(q)
    ow_exchange.start()

    local["wk"].wait()
    local["wv"].wait()
    keys = jnp.zeros((T, z.Hd), F32)
    values = jnp.zeros((T, z.Hd), F32)
    for b in range(n_e):
        block = mem_all[b]
        keys = keys + dot(block, wk[b * F : (b + 1) * F, :])
        values = values + dot(block, wv[b * F : (b + 1) * F, :])

    r_out = iota((2 * T, 2 * T), 0)
    r_in = iota((2 * T, 2 * T), 1)
    place = (
        ((r_out >> 3) & 1) * T + ((r_out >> 1) & 3) * z.L + ((r_out >> 4) << 1) + (r_out & 1)
    )
    order = (r_in == place).astype(BF16)

    middle_me = me % 2 == (me // 4 + c) % 2
    my_middle = me // 2

    def middle_dp(m):
        return 2 * m + (m // 2 + c) % 2

    class Relay:
        def __init__(self, send_buf, held, sorted_buf, recv_buf):
            self.send_buf, self.held, self.sorted_buf, self.recv_buf = (
                send_buf, held, sorted_buf, recv_buf,
            )
            self.out, self.back = sems(1), sems(1)
            self.ks_out, self.ks_back = send_sem(), send_sem()

        def each_middle(self, action):
            def step(kk, carry):
                m = (my_middle + kk) % z.mids

                @pl.when(middle_dp(m) != me)
                def _():
                    action(m)

                return carry

            lax.fori_loop(0, z.mids, step, 0)

        def first(self, m):
            copy(
                rows16(self.send_buf, m), rows16(self.held, me), self.ks_out, self.out,
                middle_dp(m), e,
            ).start()

        def start(self):
            self.each_middle(self.first)

            @pl.when(middle_me)
            def _():
                rows16(self.held, me)[...] = rows16(self.send_buf, my_middle)[...]

        def turn(self, transposed):
            @pl.when(middle_me)
            def _():
                arrive(some16(self.held)(0, n_dp - 1), self.out)
                self.sorted_buf[...] = dot(
                    relay_plan[...], self.held[...], 0 if transposed else 1, 0
                ).astype(BF16)

                def step(kk, carry):
                    j = (me + kk) % n_dp
                    copy(
                        rows16(self.sorted_buf, j), rows16(self.recv_buf, my_middle),
                        self.ks_back, self.back, j, e,
                    ).start()
                    return carry

                lax.fori_loop(1, n_dp, step, 0)
                rows16(self.recv_buf, my_middle)[...] = rows16(self.sorted_buf, me)[...]

        def end(self):
            @pl.when(middle_me)
            def _():
                arrive(some16(self.recv_buf)(0, z.mids - 1), self.back)

            @pl.when(jnp.logical_not(middle_me))
            def _():
                arrive(self.recv_buf, self.back)

        def finish(self):
            @pl.when(middle_me)
            def _():
                sent(some16(self.send_buf)(0, z.mids - 1), self.ks_out)
                sent(some16(self.sorted_buf)(0, n_dp - 1), self.ks_back)

            @pl.when(jnp.logical_not(middle_me))
            def _():
                sent(self.send_buf, self.ks_out)

    both = jnp.concatenate([keys.astype(BF16), values.astype(BF16)], axis=0)
    kv_send[...] = dot(order, both).astype(BF16)
    relay = Relay(kv_send, mid_buf, mid_out_buf, kv_recv)
    relay.start()

    meta_spread.wait()
    notes = meta[...]
    span = n_dp * TILE
    pick = ((iota((span, n_dp), 0) >> 4) == iota((span, n_dp), 1)).astype(BF16)
    spread_notes = dot(pick, notes.astype(BF16))
    wanted = ((iota((span, LANES), 0) >> 1) & 3) == iota((span, LANES), 1)
    source = jnp.sum(jnp.where(wanted, spread_notes, 0.0), axis=1, keepdims=True).astype(jnp.int32)
    p_row = iota((span, span), 0)
    p_col = iota((span, span), 1)
    relay_plan[...] = (p_col == (source * TILE + (p_row & (TILE - 1)))).astype(BF16)
    relay.turn(False)

    g_spread.wait()
    g_gather = Gather(g_all, lambda q: 0, R)
    g_gather.start(0)

    key_length = jnp.zeros((1, T), F32)
    key_at = iota((1, T), 1)
    n_row, n_lane = iota((n_dp, LANES), 0), iota((n_dp, LANES), 1)
    for k in range(z.S):
        here = jnp.logical_and(n_row == src_ref[k], n_lane == z.S + k)
        found = jnp.sum(jnp.where(here, notes, 0.0), axis=1, keepdims=True)
        found = jnp.sum(found, axis=0, keepdims=True)
        key_length = jnp.where((key_at >> log2(z.L)) == k, found, key_length)

    relay.end()
    kv = dot(order, kv_recv[...], 0, 0).astype(BF16)
    key_heads, value_heads = kv[:T], kv[T:]

    scaling = z.Hd ** (-0.5)
    same = (iota((T, T), 0) >> log2(z.L)) == (iota((T, T), 1) >> log2(z.L))
    inside = (key_at & (z.L - 1)).astype(F32) < key_length
    open_keys = jnp.logical_and(same, inside)
    scores = jnp.where(open_keys, dot(queries, key_heads, 1, 1) * scaling, -1e30)
    exps = jnp.exp(scores - jnp.max(scores, axis=1, keepdims=True))
    probabilities = exps / jnp.sum(exps, axis=1, keepdims=True)
    weights = probabilities.astype(BF16)
    att_all[e] = dot(weights, value_heads).astype(BF16)
    att_gather = Gather(att_all, lambda q: 0, T)
    att_gather.start(0)
    att_gather.mid(0)
    g_gather.mid(0)
    ow_exchange.wait()
    att_gather.end(0)

    heads_sum = jnp.zeros((T, F), F32)
    for b in range(n_e):
        heads_sum = heads_sum + dot(att_all[b], ow_all[b])
    hidden = (tok[:, pl.ds(col_e, F)].astype(F32) + heads_sum).astype(BF16).astype(F32)
    hid[...] = hidden
    part_sum = jnp.sum(hidden, axis=1, keepdims=True)
    off = hidden - part_sum * (1.0 / F)
    part_sq = jnp.sum(off * off, axis=1, keepdims=True)
    stat1[e] = to_rows([part_sum, part_sq])
    stat1_exchange = Exchange(lambda peer: stat1.at[e], lambda b: stat1.at[b], stat1)
    stat1_exchange.start()
    g_gather.end(0)
    stat1_exchange.wait()
    parts = [stat1[b] for b in range(n_e)]
    mean_row = sum(p[0:1] for p in parts) * (1.0 / D)
    square_row = sum(p[1:2] for p in parts)
    for p in parts:
        shift = p[0:1] * (1.0 / F) - mean_row
        square_row = square_row + F * (shift * shift)
    rstd_row = lax.rsqrt(square_row * (1.0 / D) + EPS)
    mean, rstd = to_columns(stack_rows(mean_row, rstd_row), 2)
    gain = fgain_ref[:, pl.ds(col_e, F)]
    unit = (hidden - mean) * rstd
    expert_in = (unit * gain).astype(BF16)
    unit_bf = unit.astype(BF16)

    x_send[...] = dot(plan[...], expert_in).astype(BF16)
    x_all[e, own_rows, :] = x_send[own_rows, :]
    x_spread = Spread(
        lambda t: rows16(x_send, t), lambda i: rows16(x_all.at[e], i), some16(x_all.at[e]), True
    )
    x_spread.start()
    local["wr"].wait()
    router = wr[...]
    lg_all[e] = dot(router, expert_in, 1, 1)
    lg_exchange = Exchange(lambda peer: lg_all.at[e], lambda b: lg_all.at[b], lg_all)
    lg_exchange.start()

    def unit_part(head):
        uw_send[head] = dot(unit_bf, ow_all[head], 1, 1)

    uw_exchange = Exchange(lambda peer: uw_send.at[peer], lambda b: uw_recv.at[b], uw_recv)
    uw_exchange.start(unit_part)
    uw_recv[e] = dot(unit_bf, ow_all[e], 1, 1)

    local["down"].wait()

    def down_back(q, carry):
        piece = pl.ds(pl.multiple_of(q * Q, Q), Q)
        total = jnp.zeros((Q, z.H), F32)
        for b in range(n_e):
            total = total + dot(g_all[b, piece, :], down[:, b * F : (b + 1) * F], 1, 1)
        u_buf[piece, :] = total
        return carry

    lax.fori_loop(0, 2, down_back, 0)

    lg_exchange.wait()
    logits = sum(lg_all[b] for b in range(n_e))
    chosen = [jnp.sum(jnp.where(h, logits, 0.0), axis=0, keepdims=True) for h in hot_rows]
    top = jnp.maximum(chosen[0], chosen[1])
    lifted = [jnp.exp(v - top) for v in chosen]
    share = [v / (lifted[0] + lifted[1]) for v in lifted]
    rank_lane = [
        (iota((T, LANES), 1) == rank[i].astype(jnp.int32)).astype(F32) for i in range(2)
    ]
    gate_rows = jnp.zeros((z.E, LANES), F32)
    for i in range(2):
        gate_rows = gate_rows + dot(jnp.where(hot_rows[i], share[i], 0.0), rank_lane[i], 1, 0, HI)
    gate_send[...] = gate_rows
    gate_recv[pl.ds(me, 1), :] = gate_send[pl.ds(me, 1), :]
    gate_spread = Spread(
        lambda t: one_row(gate_send, t), lambda i: one_row(gate_recv, i), some_rows(gate_recv)
    )
    gate_spread.start()
    lax.fori_loop(2, GROUPS, down_back, 0)

    def group_first(k):
        return ((my_group + GROUPS - k) % GROUPS) * Q

    x_gather = Gather(x_all, group_first, Q)
    local["up"].wait()
    reduces = []

    def expert_group(k):
        first = group_first(k)
        piece = pl.ds(pl.multiple_of(first, Q), Q)
        pre = jnp.zeros((Q, z.H), F32)
        for b in range(n_e):
            pre = pre + dot(x_all[b, piece, :], up[b * F : (b + 1) * F, :])
        cubic = pre * pre * pre
        slope_in = 0.7978845608028654 * (pre + 0.044715 * cubic)
        bend = jnp.tanh(slope_in)
        act = (pre * (0.5 * (1.0 + bend))).astype(BF16)
        act_buf[piece, :] = act
        slope = 0.5 * (1.0 + bend) + 0.5 * pre * (1.0 - bend * bend) * (
            0.7978845608028654 * (1.0 + 3.0 * 0.044715 * pre * pre)
        )
        grads = u_buf[piece, :]
        gates, pick, wanted = gate_column(first, Q)
        pg_buf[piece, :] = (gates * grads * slope).astype(BF16)
        dots = jnp.sum(act.astype(F32) * grads, axis=1, keepdims=True)
        return dot(pick, jnp.where(wanted, dots, 0.0), 0, 0, HI)

    def gate_column(first, rows):
        pick = (((iota((rows, n_dp), 0) + first) >> 4) == iota((rows, n_dp), 1)).astype(F32)
        wanted = (iota((rows, LANES), 0) & (CAP - 1)) == iota((rows, LANES), 1)
        spread_gates = dot(pick, gate_recv[...], 1, 0, HI)
        gates = jnp.sum(jnp.where(wanted, spread_gates, 0.0), axis=1, keepdims=True)
        return gates, pick, wanted

    def input_partial(first):
        def partial(block):
            piece = pl.ds(pl.multiple_of(first, Q), Q)
            rows = pl.ds(pl.multiple_of(block * F, F), F)
            return dot(pg_buf[piece, :], up[rows, :], 1, 1)

        return partial

    ret_spread = Spread(
        lambda t: rows16(ret_send, t), lambda i: rows16(ret_recv, i), some16(ret_recv)
    )
    bufs = (sib_send, sib_recv, own_sum, xs_send, xs_recv)

    def give_back(k):
        first = group_first(k)
        piece = pl.ds(pl.multiple_of(first, Q), Q)
        ret_send[piece, :] = reduces[k].total().astype(BF16)
        ret_spread.start_group((my_group + GROUPS - k) % GROUPS, k)

    gg_total = jnp.zeros((n_dp, LANES), F32)
    for step in range(GROUPS + 2):
        if step < GROUPS:
            x_spread.wait_group((my_group + GROUPS - step) % GROUPS, step)
            x_gather.start(step)
        if 1 <= step < GROUPS + 1:
            x_gather.mid(step - 1)
        if step == 2:
            gate_spread.wait()
        if step >= 2:
            k = step - 2
            x_gather.end(k)
            gg_total = gg_total + expert_group(k)
            reduces.append(Reduce(group_first(k), Q, input_partial(group_first(k)), bufs))
            reduces[k].local()
            reduces[k].pairs()

    gg_all[e] = gg_total
    gg_exchange = Exchange(lambda peer: gg_all.at[e], lambda b: gg_all.at[b], gg_all)
    gg_exchange.start()

    def up_back(b, carry):
        rows = pl.ds(pl.multiple_of(b * F, F), F)
        ug[rows, :] = dot(x_all[b], pg_buf[...], 0, 0).astype(BF16)
        return carry

    gates_all = gate_column(0, R)[0]

    def down_grad(b, carry):
        columns = pl.ds(pl.multiple_of(b * F, F), F)
        scaled = (g_all[b].astype(F32) * gates_all).astype(BF16)
        dg[:, columns] = dot(act_buf[...], scaled, 0, 0).astype(BF16)
        return carry

    give_back(0)
    gg_exchange.wait()
    gg_sum = sum(gg_all[b] for b in range(n_e))
    gg_send[...] = gg_sum
    gg_recv[pl.ds(me, 1), :] = gg_send[pl.ds(me, 1), :]
    gg_spread = Spread(
        lambda t: one_row(gg_send, t), lambda i: one_row(gg_recv, i), some_rows(gg_recv)
    )
    gg_spread.start()
    give_back(1)
    lax.fori_loop(0, n_e // 2, up_back, 0)
    give_back(2)
    lax.fori_loop(n_e // 2, n_e, up_back, 0)
    give_back(3)
    ret_recv[own_rows, :] = ret_send[own_rows, :]
    up_store = pltpu.make_async_copy(ug, up_out, ls.at[len(local)])
    up_store.start()
    lax.fori_loop(0, n_e // 2, down_grad, 0)

    gg_spread.wait()
    gate_grad = []
    for i in range(2):
        spread_gg = dot(gg_recv[...], rank_lane[i], 1, 1, HI)
        gate_grad.append(jnp.sum(jnp.where(hot_rows[i], spread_gg, 0.0), axis=0, keepdims=True))
    delta = share[0] * share[1] * (gate_grad[0] - gate_grad[1])
    logit_grad = jnp.where(hot_rows[0], delta, 0.0) - jnp.where(hot_rows[1], delta, 0.0)
    high = logit_grad.astype(BF16)
    low = (logit_grad - high.astype(F32)).astype(BF16)
    router_term = dot(high, router, 0, 0) + dot(low, router, 0, 0)
    share_columns = to_columns(stack_rows(share[0], share[1]), 2)

    ret_spread.wait()
    returned = ret_recv[...]
    ffn_in_grad = (
        share_columns[0] * dot(plan0[...], returned)
        + share_columns[1] * dot(plan1[...], returned)
        + router_term
    )

    scaled_in = ffn_in_grad * gain
    unit = (hid[...] - mean) * rstd
    stat2[e] = to_rows(
        [
            jnp.sum(scaled_in, axis=1, keepdims=True),
            jnp.sum(scaled_in * unit, axis=1, keepdims=True),
        ]
    )
    stat2_exchange = Exchange(lambda peer: stat2.at[e], lambda b: stat2.at[b], stat2)
    stat2_exchange.start()
    hg_all[e] = (live[...].astype(F32) + rstd * scaled_in).astype(BF16)
    hg_gather = Gather(hg_all, lambda q: q * (T // 2), T // 2)
    hg_gather.start(0)
    hg_gather.start(1)
    lax.fori_loop(n_e // 2, n_e, down_grad, 0)
    down_store = pltpu.make_async_copy(dg, down_out, ls.at[len(local) + 1])
    down_store.start()
    uw_exchange.wait()
    unit_heads = sum(uw_recv[b] for b in range(n_e))
    weight_sums = dot(jnp.ones((8, D), BF16), wo[...], 1, 1)[:1]
    hg_gather.mid(0)
    hg_gather.mid(1)
    stat2_exchange.wait()
    sums = sum(stat2[b] for b in range(n_e)) * (1.0 / D)
    mean_in, mean_unit = to_columns(sums, 2)
    hg_gather.end(0)
    hg_gather.end(1)

    att_grad = jnp.zeros((T, z.Hd), F32)
    for b in range(n_e):
        att_grad = att_grad + dot(hg_all[b], wo[:, b * F : (b + 1) * F], 1, 1)
    att_grad = att_grad - (rstd * mean_in) * weight_sums - (rstd * mean_unit) * unit_heads
    att_grad = att_grad.astype(BF16)
    value_grad = dot(weights, att_grad, 0, 0).astype(BF16)
    prob_grad = dot(att_grad, value_heads, 1, 1)
    inner = jnp.sum(probabilities * prob_grad, axis=1, keepdims=True)
    score_grad = (probabilities * (prob_grad - inner) * scaling).astype(BF16)
    key_grad = dot(score_grad, queries, 0, 0).astype(BF16)
    both = jnp.concatenate([key_grad, value_grad], axis=0)
    kvg_send[...] = dot(order, both).astype(BF16)
    relay_back = Relay(kvg_send, mid_buf2, mid_out2, kvg_recv)
    relay_back.start()
    relay_back.turn(True)
    relay_back.end()
    home = dot(order, kvg_recv[...], 0, 0).astype(BF16)
    home_keys, home_values = home[:T], home[T:]

    def memory_partial(block):
        rows = pl.ds(pl.multiple_of(block * F, F), F)
        return dot(home_keys, wk[rows, :], 1, 1) + dot(home_values, wv[rows, :], 1, 1)

    def memory_send(block):
        mg_send[block] = memory_partial(block).astype(BF16)

    memory_exchange = Exchange(lambda peer: mg_send.at[peer], lambda b: mg_recv.at[b], mg_recv)
    memory_exchange.start(memory_send)
    mg_recv[e] = jnp.zeros((T, F), BF16)
    own_part = memory_partial(e)
    memory_exchange.wait()
    mg[...] = (own_part + sum(mg_recv[b].astype(F32) for b in range(n_e))).astype(BF16)
    mem_store = pltpu.make_async_copy(mg, mem_out, ls.at[len(local) + 2])
    mem_store.start()

    relay.finish()
    relay_back.finish()
    for finish in pending:
        finish()
    up_store.wait()
    down_store.wait()
    mem_store.wait()
    assert counter[0] <= SEMS and counter[1] <= SENDS, counter


SEMS = 80
SENDS = 32


def hand_on(*refs):
    arrays, results, held = refs[0:3], refs[3:6], refs[6:9]
    in_sem, out_sem = refs[9:]
    pieces = []
    for a in range(3):
        rows = arrays[a].shape[0]
        cuts = 8 if rows >= 512 else 1
        for j in range(cuts):
            pieces.append((a, pl.ds(j * (rows // cuts), rows // cuts)))

    def step(source, target, i, sem):
        a, piece = pieces[i]
        return pltpu.make_async_copy(source[a].at[piece], target[a].at[piece], sem.at[i])

    for i in range(len(pieces)):
        step(arrays, held, i, in_sem).start()
    for i in range(len(pieces)):
        step(arrays, held, i, in_sem).wait()
        step(held, results, i, out_sem).start()
    for i in range(len(pieces)):
        step(held, results, i, out_sem).wait()


def build(mesh):
    n_dp, n_e = mesh.shape["dp"], mesh.shape["expert"]

    def body(
        tokens, memory, source_length, owner_device, source_device, target_length, routing,
        attn_gain, ffn_gain, query_weight, key_weight, value_weight, out_weight, router_weight,
        up_weight, down_weight, grad_out,
    ):
        sentences, length, width = tokens.shape
        z = Layout(
            n_dp, n_e, sentences, length, width, query_weight.shape[1], up_weight.shape[2],
            router_weight.shape[1],
        )
        T, D, F, R, H = z.T, z.D, z.F, z.R, z.H
        span = n_dp * TILE
        vm = pltpu.VMEM
        scratch = [
            vm((T, D), BF16), vm((T, F), BF16), vm((D, z.Hd), BF16), vm((D, z.Hd), BF16),
            vm((D, z.Hd), BF16), vm((z.Hd, D), BF16), vm((z.E, F), BF16), vm((D, H), BF16),
            vm((H, D), BF16),
            vm((n_e, T, F), BF16), vm((n_e, z.Hd, F), BF16), vm((n_e, T, z.Hd), BF16),
            vm((n_e, T, F), BF16), vm((n_e, R, F), BF16), vm((n_e, R, F), BF16),
            vm((R, F), BF16), vm((R, F), BF16), vm((R, F), BF16), vm((R, F), BF16),
            vm((n_dp, LANES), F32),
            vm((2 * T, z.Hd), BF16), vm((span, z.Hd), BF16), vm((span, z.Hd), BF16),
            vm((2 * T, z.Hd), BF16),
            vm((2 * T, z.Hd), BF16), vm((span, z.Hd), BF16), vm((span, z.Hd), BF16),
            vm((2 * T, z.Hd), BF16),
            vm((n_e, 8, T), F32), vm((n_e, 8, T), F32), vm((n_e, z.E, T), F32),
            vm((z.E, LANES), F32), vm((n_dp, LANES), F32), vm((n_e, n_dp, LANES), F32),
            vm((n_dp, LANES), F32), vm((n_dp, LANES), F32),
            vm((R, T), BF16), vm((T, R), BF16), vm((T, R), BF16), vm((span, span), BF16),
            vm((R, H), F32), vm((R, H), BF16), vm((R, H), BF16),
            vm((4, R, F), BF16), vm((4, R, F), BF16), vm((R, F), F32), vm((3, R, F), BF16),
            vm((3, R, F), BF16), vm((n_e, T, z.Hd), F32), vm((n_e, T, z.Hd), F32),
            vm((n_e, T, F), BF16), vm((n_e, T, F), BF16),
            vm((D, H), BF16), vm((H, D), BF16), vm((T, F), BF16), vm((T, F), F32),
            pltpu.SemaphoreType.DMA((SENDS,)), pltpu.SemaphoreType.DMA((SEMS,)),
            pltpu.SemaphoreType.DMA((16,)),
        ]
        smem = pl.BlockSpec(memory_space=pltpu.SMEM)
        vmem = pl.BlockSpec(memory_space=pltpu.VMEM)
        hbm = pl.BlockSpec(memory_space=pl.ANY)
        results = pl.pallas_call(
            functools.partial(layer_kernel, z),
            out_shape=(
                jax.ShapeDtypeStruct((T, F), BF16),
                jax.ShapeDtypeStruct((D, H), BF16),
                jax.ShapeDtypeStruct((H, D), BF16),
            ),
            in_specs=[smem] * 3 + [vmem] * 3 + [hbm] * 10,
            out_specs=(hbm, hbm, hbm),
            scratch_shapes=scratch,
            compiler_params=pltpu.CompilerParams(
                collective_id=0, has_side_effects=True, vmem_limit_bytes=56 * 1024 * 1024
            ),
            name="layer",
        )(
            source_device, source_length, target_length, jnp.transpose(routing, (0, 2, 1)),
            attn_gain[None], ffn_gain[None],
            tokens.reshape(T, D), memory.reshape(T, F), grad_out.reshape(T, D),
            query_weight, key_weight, value_weight, out_weight, router_weight.T,
            up_weight[0], down_weight[0],
        )
        mem_grad, up_grad, down_grad = pl.pallas_call(
            hand_on,
            out_shape=tuple(jax.ShapeDtypeStruct(r.shape, r.dtype) for r in results),
            in_specs=[hbm] * 3,
            out_specs=(hbm, hbm, hbm),
            scratch_shapes=[pltpu.VMEM(r.shape, r.dtype) for r in results]
            + [pltpu.SemaphoreType.DMA((17,)), pltpu.SemaphoreType.DMA((17,))],
            compiler_params=pltpu.CompilerParams(vmem_limit_bytes=56 * 1024 * 1024),
            name="hand_on",
        )(*results)
        return mem_grad.reshape(sentences, length, F), up_grad[None], down_grad[None]

    return body


def solution(mesh):
    in_specs = (
        P("dp", None, None),
        P("dp", None, "expert"),
        P("dp"),
        P("dp"),
        P("dp"),
        P("dp"),
        P("dp", None, None),
        P(),
        P(),
        P(None, "expert"),
        P(None, "expert"),
        P(None, "expert"),
        P("expert", None),
        P(),
        P("dp", None, "expert"),
        P("dp", "expert", None),
        P("dp", None, None),
    )
    out_specs = (P("dp", None, "expert"), P("dp", None, "expert"), P("dp", "expert", None))
    return jax.shard_map(
        build(mesh), mesh=mesh, in_specs=in_specs, out_specs=out_specs, check_vma=False
    )
```

time: 151 us -> 128 us (0.85); the launches traced: 149 us -> 128 us
  Pallas kernels: 139 us -> 127 us
  local copies, waits for them, and re-layouts: 9.31 us -> 0 us
    pallas_call x1, Pallas kernels: 139 us -> 123 us  [body(): pl.pallas_call(functools.partial(layer_kernel, z), out_shape=(jax.ShapeDt...]
    unnamed x7 -> x0, local copies, waits for them, and re-layouts: 9.31 us -> none
    pallas_call x0 -> x1, Pallas kernels: none -> 3.95 us  [body(): pl.pallas_call(hand_on, out_shape=tuple((jax.ShapeDtypeStruct(r.shape, r....]
where the time goes in v2:
time: 128 us
  Pallas kernels  127 us (99%)
    pallas_call x1, Pallas kernels, body(): pl.pallas_call(functools.partial(layer_kernel, z), out_shape=(jax.ShapeDt...  123 us
    pallas_call x1, Pallas kernels, body(): pl.pallas_call(hand_on, out_shape=tuple((jax.ShapeDtypeStruct(r.shape, r....  3.95 us

profile of v2, /device:TPU:1, one launch (start us, length us, event | category | flops | bytes accessed | tf_op | source)
XLA Modules:
  0.0 127.6 jit_solution(17323784321739125868)
XLA Ops:
  0.6 122.9 %layer.1 = (bf16[128,256]{1,0:T(8,128)(2,1)}, bf16[2048,512]{1,0:T(8,128)(2,1)}, bf16[512,2048]{1,0:T(8,128)(2,1)}) custom-call(s32[4]{0:T(128)} %src_ref.1, s32[4]{0:T(128)} %slen_ref.1, s32[4]{0:T(128)} %tlen_ref.1, s32[4,2,32]{2,1,0:T(2,128)} %bitcast.20, f32[1,2048]{1,0:T(1,128)} %bitcast.18, f32[1,2048]{1,0:T(1,128)} %bitcast.19, ...), custom_call_target="tpu_custom_call" | custom-call | tf_op jit(solution)/shard_map/layer/pallas_call | solution.py:852
  123.5 4.0 %hand_on.1 = (bf16[128,256]{1,0:T(8,128)(2,1)}, bf16[2048,512]{1,0:T(8,128)(2,1)}, bf16[512,2048]{1,0:T(8,128)(2,1)}) custom-call(bf16[128,256]{1,0:T(8,128)(2,1)} %get-tuple-element.9.refs_0_, bf16[2048,512]{1,0:T(8,128)(2,1)} %get-tuple-element.10.refs_1_, bf16[512,2048]{1,0:T(8,128)(2,1)} %get-tuple-element.11.refs_2_), custom_call_target="tpu_custom_call" | custom-call | tf_op jit(solution)/shard_map/hand_on/pallas_call | solution.py:873

commit v3 on v2

--- a/solution.py
+++ b/solution.py
@@ -68,12 +68,12 @@
     tokens_hbm, memory_hbm, grad_hbm, wq_hbm, wk_hbm, wv_hbm, wo_hbm, wr_hbm, up_hbm, down_hbm,
     mem_out, up_out, down_out,
     tok, live, wq, wk, wv, wo, wr, up, down,
-    mem_all, ow_all, att_all, hg_all, x_all, g_all,
+    mem_all, ow_all, att_all, ag_send, ag_recv, x_all, g_all,
     g_send, x_send, ret_send, ret_recv,
     meta, kv_send, mid_buf, mid_out_buf, kv_recv, kvg_send, mid_buf2, mid_out2, kvg_recv,
     stat1, stat2, lg_all, gate_send, gate_recv, gg_all, gg_send, gg_recv,
     plan, plan0, plan1, relay_plan, u_buf, act_buf, pg_buf,
-    sib_send, sib_recv, own_sum, xs_send, xs_recv, uw_send, uw_recv, mg_send, mg_recv,
+    sib_send, sib_recv, own_sum, held_sum, xs_send, far_recv, xs_recv, uw_send, uw_recv, mg_send, mg_recv,
     ug, dg, mg, hid,
     ss, rs, ls,
 ):
@@ -162,8 +162,8 @@
             arrive(self.some(0, n_dp - 1), self.base)
 
     class Gather:
-        def __init__(self, ref, first, rows):
-            self.ref, self.first, self.rows = ref, first, rows
+        def __init__(self, ref, first, rows, ringed=0):
+            self.ref, self.first, self.rows, self.ringed = ref, first, rows, ringed
             self.parts = ref.shape[1] // rows
             self.ks = send_sem()
             self.base = sems(4 * self.parts)
@@ -177,15 +177,24 @@
             copy(ref, ref, self.ks, self.base + 4 * q + t, me, peer).start()
 
         def start(self, q):
-            self.go(q, 2, e, across)
+            if q >= self.ringed:
+                self.go(q, 2, e, across)
             self.go(q, 0, e, right)
             self.go(q, 1, e, left)
             self.go(q, 3, e, sib)
 
         def mid(self, q):
-            for t, block in ((0, left), (1, right), (2, across)):
+            for t, block, onward in ((0, left, right), (1, right, left)):
                 arrive(self.part(block, q), self.base + 4 * q + t)
+                if q < self.ringed and t == q % 2:
+                    self.go(q, 2, block, onward)
                 self.go(q, 3, block, sib)
+            if q >= self.ringed:
+                self.far(q)
+
+        def far(self, q):
+            arrive(self.part(across, q), self.base + 4 * q + 2)
+            self.go(q, 3, across, sib)
 
         def end(self, q):
             four = self.ref.at[pl.ds(0, 4), pl.ds(pl.multiple_of(self.first(q), TILE), self.rows)]
@@ -214,11 +223,11 @@
             arrive(self.ref.at[pl.ds(0, n_e - 1)], self.base)
 
     class Reduce:
-        def __init__(self, first, n, partial, bufs):
-            self.n, self.partial, self.first = n, partial, first
-            self.sib_send, self.sib_recv, self.own, self.xs, self.landing = bufs
+        def __init__(self, first, n, partial, bufs, ring=None):
+            self.n, self.partial, self.first, self.ring = n, partial, first, ring
+            self.sib_send, self.sib_recv, self.own, self.held, self.xs, self.far, self.landing = bufs
             self.ks = send_sem()
-            self.base = sems(5)
+            self.base = sems(6)
             sent_later(x_all.at[pl.ds(0, 7), pl.ds(0, n)], self.ks)
 
         def piece(self):
@@ -232,7 +241,13 @@
                 theirs = self.sib_recv.at[dx, self.piece()]
                 copy(mine, theirs, self.ks, self.base + dx, me, sib).start()
 
+        def put(self, dx, value, landing, there, t):
+            out = self.xs.at[dx - 1, self.piece()]
+            out[...] = value.astype(BF16)
+            copy(out, landing, self.ks, self.base + t, me, there).start()
+
         def pairs(self):
+            waits = {None: None, 0: 1, 1: 3}[self.ring]
             for dx in (2, 1, 3, 0):
                 there = 2 * ((x + dx) % 4) + c
                 own = self.partial(there)
@@ -241,18 +256,33 @@
                 both = own + theirs[...].astype(F32)
                 if dx == 0:
                     self.own[self.piece(), :] = both
+                elif dx == waits:
+                    self.held[self.piece(), :] = both
+                elif dx == 2 and self.ring is not None:
+                    by = left if self.ring else right
+                    self.put(dx, both, self.far.at[self.piece()], by, 5)
                 else:
-                    out = self.xs.at[dx - 1, self.piece()]
-                    out[...] = both.astype(BF16)
-                    to = self.landing.at[dx - 1, self.piece()]
-                    copy(out, to, self.ks, self.base + 4, me, there).start()
+                    self.put(dx, both, self.landing.at[dx - 1, self.piece()], there, 4)
+
+        def onward(self):
+            dx, there = (3, left) if self.ring else (1, right)
+            arrive(self.far.at[self.piece()], self.base + 5)
+            both = self.held[self.piece(), :] + self.far[self.piece(), :].astype(F32)
+            self.put(dx, both, self.landing.at[dx - 1, self.piece()], there, 4)
 
         def total(self):
-            arrive(self.landing.at[pl.ds(0, 3), self.piece()], self.base + 4)
+            parts = (0, 1, 2) if self.ring is None else (0, 2)
+            arrive(self.landing.at[pl.ds(0, len(parts)), self.piece()], self.base + 4)
             value = self.own[self.piece(), :]
-            for i in range(3):
+            for i in parts:
                 value = value + self.landing[i, self.piece(), :].astype(F32)
             return value
+
+    def group(k):
+        return (my_group + GROUPS - k) % GROUPS
+
+    def group_first(k):
+        return group(k) * Q
 
     local = {}
 
@@ -330,9 +360,11 @@
     meta_spread = Spread(lambda t: one_row(meta, me), lambda i: one_row(meta, i), some_rows(meta))
     meta_spread.start()
     g_spread = Spread(
-        lambda t: rows16(g_send, t), lambda i: rows16(g_all.at[e], i), some16(g_all.at[e])
-    )
-    g_spread.start()
+        lambda t: rows16(g_send, t), lambda i: rows16(g_all.at[e], i), some16(g_all.at[e]), True
+    )
+    g_gather = Gather(g_all, group_first, Q)
+    for k in range(2):
+        g_spread.start_group((my_group + k) % GROUPS, k)
 
     local["tokens"].wait()
     local["wq"].wait()
@@ -468,11 +500,13 @@
     p_row = iota((span, span), 0)
     p_col = iota((span, span), 1)
     relay_plan[...] = (p_col == (source * TILE + (p_row & (TILE - 1)))).astype(BF16)
+    for k in range(2):
+        g_spread.wait_group(group(k), k)
+        g_gather.start(k)
     relay.turn(False)
-
-    g_spread.wait()
-    g_gather = Gather(g_all, lambda q: 0, R)
-    g_gather.start(0)
+    for k in range(2, GROUPS):
+        g_spread.start_group((my_group + k) % GROUPS, k)
+    g_gather.mid(0)
 
     key_length = jnp.zeros((1, T), F32)
     key_at = iota((1, T), 1)
@@ -498,8 +532,10 @@
     att_all[e] = dot(weights, value_heads).astype(BF16)
     att_gather = Gather(att_all, lambda q: 0, T)
     att_gather.start(0)
+    g_gather.mid(1)
+    g_spread.wait_group(group(2), 2)
+    g_gather.start(2)
     att_gather.mid(0)
-    g_gather.mid(0)
     ow_exchange.wait()
     att_gather.end(0)
 
@@ -514,8 +550,10 @@
     stat1[e] = to_rows([part_sum, part_sq])
     stat1_exchange = Exchange(lambda peer: stat1.at[e], lambda b: stat1.at[b], stat1)
     stat1_exchange.start()
-    g_gather.end(0)
+    g_gather.mid(2)
     stat1_exchange.wait()
+    g_spread.wait_group(group(3), 3)
+    g_gather.start(3)
     parts = [stat1[b] for b in range(n_e)]
     mean_row = sum(p[0:1] for p in parts) * (1.0 / D)
     square_row = sum(p[1:2] for p in parts)
@@ -527,7 +565,6 @@
     gain = fgain_ref[:, pl.ds(col_e, F)]
     unit = (hidden - mean) * rstd
     expert_in = (unit * gain).astype(BF16)
-    unit_bf = unit.astype(BF16)
 
     x_send[...] = dot(plan[...], expert_in).astype(BF16)
     x_all[e, own_rows, :] = x_send[own_rows, :]
@@ -541,24 +578,27 @@
     lg_exchange = Exchange(lambda peer: lg_all.at[e], lambda b: lg_all.at[b], lg_all)
     lg_exchange.start()
 
-    def unit_part(head):
-        uw_send[head] = dot(unit_bf, ow_all[head], 1, 1)
-
-    uw_exchange = Exchange(lambda peer: uw_send.at[peer], lambda b: uw_recv.at[b], uw_recv)
-    uw_exchange.start(unit_part)
-    uw_recv[e] = dot(unit_bf, ow_all[e], 1, 1)
-
     local["down"].wait()
 
-    def down_back(q, carry):
-        piece = pl.ds(pl.multiple_of(q * Q, Q), Q)
+    def down_back(k):
+        piece = pl.ds(pl.multiple_of(group_first(k), Q), Q)
         total = jnp.zeros((Q, z.H), F32)
         for b in range(n_e):
             total = total + dot(g_all[b, piece, :], down[:, b * F : (b + 1) * F], 1, 1)
         u_buf[piece, :] = total
-        return carry
-
-    lax.fori_loop(0, 2, down_back, 0)
+
+    x_gather = Gather(x_all, group_first, Q, 2)
+
+    def x_start(k):
+        x_spread.wait_group(group(k), k)
+        x_gather.start(k)
+
+    g_gather.end(0)
+    down_back(0)
+    x_start(0)
+    g_gather.end(1)
+    down_back(1)
+    x_start(1)
 
     lg_exchange.wait()
     logits = sum(lg_all[b] for b in range(n_e))
@@ -578,12 +618,14 @@
         lambda t: one_row(gate_send, t), lambda i: one_row(gate_recv, i), some_rows(gate_recv)
     )
     gate_spread.start()
-    lax.fori_loop(2, GROUPS, down_back, 0)
-
-    def group_first(k):
-        return ((my_group + GROUPS - k) % GROUPS) * Q
-
-    x_gather = Gather(x_all, group_first, Q)
+    g_gather.mid(3)
+    g_gather.end(2)
+    down_back(2)
+    x_start(2)
+    g_gather.end(3)
+    down_back(3)
+    x_start(3)
+
     local["up"].wait()
     reduces = []
 
@@ -602,17 +644,17 @@
             0.7978845608028654 * (1.0 + 3.0 * 0.044715 * pre * pre)
         )
         grads = u_buf[piece, :]
-        gates, pick, wanted = gate_column(first, Q)
-        pg_buf[piece, :] = (gates * grads * slope).astype(BF16)
+        steep = grads * slope
+        u_buf[piece, :] = steep
+        pg_buf[piece, :] = steep.astype(BF16)
+        pick, wanted = slot_masks(first, Q)
         dots = jnp.sum(act.astype(F32) * grads, axis=1, keepdims=True)
         return dot(pick, jnp.where(wanted, dots, 0.0), 0, 0, HI)
 
-    def gate_column(first, rows):
+    def slot_masks(first, rows):
         pick = (((iota((rows, n_dp), 0) + first) >> 4) == iota((rows, n_dp), 1)).astype(F32)
         wanted = (iota((rows, LANES), 0) & (CAP - 1)) == iota((rows, LANES), 1)
-        spread_gates = dot(pick, gate_recv[...], 1, 0, HI)
-        gates = jnp.sum(jnp.where(wanted, spread_gates, 0.0), axis=1, keepdims=True)
-        return gates, pick, wanted
+        return pick, wanted
 
     def input_partial(first):
         def partial(block):
@@ -625,41 +667,46 @@
     ret_spread = Spread(
         lambda t: rows16(ret_send, t), lambda i: rows16(ret_recv, i), some16(ret_recv)
     )
-    bufs = (sib_send, sib_recv, own_sum, xs_send, xs_recv)
+    bufs = (sib_send, sib_recv, own_sum, held_sum, xs_send, far_recv, xs_recv)
 
     def give_back(k):
         first = group_first(k)
         piece = pl.ds(pl.multiple_of(first, Q), Q)
         ret_send[piece, :] = reduces[k].total().astype(BF16)
-        ret_spread.start_group((my_group + GROUPS - k) % GROUPS, k)
+        ret_spread.start_group(group(k), k)
 
     gg_total = jnp.zeros((n_dp, LANES), F32)
-    for step in range(GROUPS + 2):
-        if step < GROUPS:
-            x_spread.wait_group((my_group + GROUPS - step) % GROUPS, step)
-            x_gather.start(step)
-        if 1 <= step < GROUPS + 1:
-            x_gather.mid(step - 1)
-        if step == 2:
-            gate_spread.wait()
-        if step >= 2:
-            k = step - 2
-            x_gather.end(k)
-            gg_total = gg_total + expert_group(k)
-            reduces.append(Reduce(group_first(k), Q, input_partial(group_first(k)), bufs))
-            reduces[k].local()
-            reduces[k].pairs()
-
-    gg_all[e] = gg_total
-    gg_exchange = Exchange(lambda peer: gg_all.at[e], lambda b: gg_all.at[b], gg_all)
-    gg_exchange.start()
+    x_gather.mid(0)
+    x_gather.mid(1)
+    x_gather.far(0)
+    for k in range(GROUPS):
+        if k + 2 < GROUPS:
+            x_gather.mid(k + 2)
+        if k == 0:
+            x_gather.far(1)
+        x_gather.end(k)
+        gg_total = gg_total + expert_group(k)
+        if k == GROUPS - 1:
+            gg_all[e] = gg_total
+            gg_exchange = Exchange(lambda peer: gg_all.at[e], lambda b: gg_all.at[b], gg_all)
+            gg_exchange.start()
+        reduces.append(
+            Reduce(group_first(k), Q, input_partial(group_first(k)), bufs, k if k < 2 else None)
+        )
+        reduces[k].local()
+        reduces[k].pairs()
+        if k in (1, 2):
+            reduces[k - 1].onward()
 
     def up_back(b, carry):
         rows = pl.ds(pl.multiple_of(b * F, F), F)
         ug[rows, :] = dot(x_all[b], pg_buf[...], 0, 0).astype(BF16)
         return carry
 
-    gates_all = gate_column(0, R)[0]
+    pick, wanted = slot_masks(0, R)
+    gate_spread.wait()
+    spread_gates = dot(pick, gate_recv[...], 1, 0, HI)
+    gates_all = jnp.sum(jnp.where(wanted, spread_gates, 0.0), axis=1, keepdims=True)
 
     def down_grad(b, carry):
         columns = pl.ds(pl.multiple_of(b * F, F), F)
@@ -677,11 +724,22 @@
     )
     gg_spread.start()
     give_back(1)
+    pg_buf[...] = (gates_all * u_buf[...]).astype(BF16)
     lax.fori_loop(0, n_e // 2, up_back, 0)
     give_back(2)
     lax.fori_loop(n_e // 2, n_e, up_back, 0)
     give_back(3)
     ret_recv[own_rows, :] = ret_send[own_rows, :]
+
+    unit_bf = ((hid[...] - mean) * rstd).astype(BF16)
+
+    def unit_part(head):
+        uw_send[head] = dot(unit_bf, ow_all[head], 1, 1).astype(BF16)
+
+    uw_exchange = Exchange(lambda peer: uw_send.at[peer], lambda b: uw_recv.at[b], uw_recv)
+    uw_exchange.start(unit_part)
+    uw_recv[e] = dot(unit_bf, ow_all[e], 1, 1).astype(BF16)
+
     up_store = pltpu.make_async_copy(ug, up_out, ls.at[len(local)])
     up_store.start()
     lax.fori_loop(0, n_e // 2, down_grad, 0)
@@ -701,8 +759,8 @@
     ret_spread.wait()
     returned = ret_recv[...]
     ffn_in_grad = (
-        share_columns[0] * dot(plan0[...], returned)
-        + share_columns[1] * dot(plan1[...], returned)
+        (share_columns[0] * share_columns[0]) * dot(plan0[...], returned)
+        + (share_columns[1] * share_columns[1]) * dot(plan1[...], returned)
         + router_term
     )
 
@@ -716,27 +774,27 @@
     )
     stat2_exchange = Exchange(lambda peer: stat2.at[e], lambda b: stat2.at[b], stat2)
     stat2_exchange.start()
-    hg_all[e] = (live[...].astype(F32) + rstd * scaled_in).astype(BF16)
-    hg_gather = Gather(hg_all, lambda q: q * (T // 2), T // 2)
-    hg_gather.start(0)
-    hg_gather.start(1)
+    sent_grad = (live[...].astype(F32) + rstd * scaled_in).astype(BF16)
+
+    def head_part(head):
+        ag_send[head] = dot(sent_grad, ow_all[head], 1, 1).astype(BF16)
+
+    ag_exchange = Exchange(lambda peer: ag_send.at[peer], lambda b: ag_recv.at[b], ag_recv)
+    ag_exchange.start(head_part)
+    ag_recv[e] = jnp.zeros((T, z.Hd), BF16)
+    att_grad = dot(sent_grad, ow_all[e], 1, 1)
     lax.fori_loop(n_e // 2, n_e, down_grad, 0)
     down_store = pltpu.make_async_copy(dg, down_out, ls.at[len(local) + 1])
     down_store.start()
     uw_exchange.wait()
-    unit_heads = sum(uw_recv[b] for b in range(n_e))
+    unit_heads = sum(uw_recv[b].astype(F32) for b in range(n_e))
     weight_sums = dot(jnp.ones((8, D), BF16), wo[...], 1, 1)[:1]
-    hg_gather.mid(0)
-    hg_gather.mid(1)
     stat2_exchange.wait()
     sums = sum(stat2[b] for b in range(n_e)) * (1.0 / D)
     mean_in, mean_unit = to_columns(sums, 2)
-    hg_gather.end(0)
-    hg_gather.end(1)
-
-    att_grad = jnp.zeros((T, z.Hd), F32)
-    for b in range(n_e):
-        att_grad = att_grad + dot(hg_all[b], wo[:, b * F : (b + 1) * F], 1, 1)
+    ag_exchange.wait()
+
+    att_grad = att_grad + sum(ag_recv[b].astype(F32) for b in range(n_e))
     att_grad = att_grad - (rstd * mean_in) * weight_sums - (rstd * mean_unit) * unit_heads
     att_grad = att_grad.astype(BF16)
     value_grad = dot(weights, att_grad, 0, 0).astype(BF16)
@@ -779,7 +837,7 @@
     assert counter[0] <= SEMS and counter[1] <= SENDS, counter
 
 
-SEMS = 80
+SEMS = 96
 SENDS = 32
 
 
@@ -827,7 +885,8 @@
             vm((D, z.Hd), BF16), vm((z.Hd, D), BF16), vm((z.E, F), BF16), vm((D, H), BF16),
             vm((H, D), BF16),
             vm((n_e, T, F), BF16), vm((n_e, z.Hd, F), BF16), vm((n_e, T, z.Hd), BF16),
-            vm((n_e, T, F), BF16), vm((n_e, R, F), BF16), vm((n_e, R, F), BF16),
+            vm((n_e, T, z.Hd), BF16), vm((n_e, T, z.Hd), BF16),
+            vm((n_e, R, F), BF16), vm((n_e, R, F), BF16),
             vm((R, F), BF16), vm((R, F), BF16), vm((R, F), BF16), vm((R, F), BF16),
             vm((n_dp, LANES), F32),
             vm((2 * T, z.Hd), BF16), vm((span, z.Hd), BF16), vm((span, z.Hd), BF16),
@@ -839,8 +898,9 @@
             vm((n_dp, LANES), F32), vm((n_dp, LANES), F32),
             vm((R, T), BF16), vm((T, R), BF16), vm((T, R), BF16), vm((span, span), BF16),
             vm((R, H), F32), vm((R, H), BF16), vm((R, H), BF16),
-            vm((4, R, F), BF16), vm((4, R, F), BF16), vm((R, F), F32), vm((3, R, F), BF16),
-            vm((3, R, F), BF16), vm((n_e, T, z.Hd), F32), vm((n_e, T, z.Hd), F32),
+            vm((4, R, F), BF16), vm((4, R, F), BF16), vm((R, F), F32), vm((R, F), F32),
+            vm((3, R, F), BF16), vm((R, F), BF16), vm((3, R, F), BF16),
+            vm((n_e, T, z.Hd), BF16), vm((n_e, T, z.Hd), BF16),
             vm((n_e, T, F), BF16), vm((n_e, T, F), BF16),
             vm((D, H), BF16), vm((H, D), BF16), vm((T, F), BF16), vm((T, F), F32),
             pltpu.SemaphoreType.DMA((SENDS,)), pltpu.SemaphoreType.DMA((SEMS,)),

time: 128 us -> 124 us (0.969)
  Pallas kernels: 127 us -> 123 us
    pallas_call x1, Pallas kernels: 123 us -> 119 us  [body(): pl.pallas_call(functools.partial(layer_kernel, z), out_shape=(jax.ShapeDt...]
where the time goes in v3:
time: 124 us
  Pallas kernels  123 us (99%)
    pallas_call x1, Pallas kernels, body(): pl.pallas_call(functools.partial(layer_kernel, z), out_shape=(jax.ShapeDt...  119 us
    pallas_call x1, Pallas kernels, body(): pl.pallas_call(hand_on, out_shape=tuple((jax.ShapeDtypeStruct(r.shape, r....  3.95 us

profile of v3, /device:TPU:1, one launch (start us, length us, event | category | flops | bytes accessed | tf_op | source)
XLA Modules:
  0.0 123.9 jit_solution(12016148910796876200)
XLA Ops:
  0.6 119.2 %layer.1 = (bf16[128,256]{1,0:T(8,128)(2,1)}, bf16[2048,512]{1,0:T(8,128)(2,1)}, bf16[512,2048]{1,0:T(8,128)(2,1)}) custom-call(s32[4]{0:T(128)} %src_ref.1, s32[4]{0:T(128)} %slen_ref.1, s32[4]{0:T(128)} %tlen_ref.1, s32[4,2,32]{2,1,0:T(2,128)} %bitcast.20, f32[1,2048]{1,0:T(1,128)} %bitcast.18, f32[1,2048]{1,0:T(1,128)} %bitcast.19, ...), custom_call_target="tpu_custom_call" | custom-call | tf_op jit(solution)/shard_map/layer/pallas_call | solution.py:912
  119.8 4.0 %hand_on.1 = (bf16[128,256]{1,0:T(8,128)(2,1)}, bf16[2048,512]{1,0:T(8,128)(2,1)}, bf16[512,2048]{1,0:T(8,128)(2,1)}) custom-call(bf16[128,256]{1,0:T(8,128)(2,1)} %get-tuple-element.9.refs_0_, bf16[2048,512]{1,0:T(8,128)(2,1)} %get-tuple-element.10.refs_1_, bf16[512,2048]{1,0:T(8,128)(2,1)} %get-tuple-element.11.refs_2_), custom_call_target="tpu_custom_call" | custom-call | tf_op jit(solution)/shard_map/hand_on/pallas_call | solution.py:933

commit v4 on v3

--- a/solution.py
+++ b/solution.py
@@ -587,7 +587,7 @@
             total = total + dot(g_all[b, piece, :], down[:, b * F : (b + 1) * F], 1, 1)
         u_buf[piece, :] = total
 
-    x_gather = Gather(x_all, group_first, Q, 2)
+    x_gather = Gather(x_all, group_first, Q, 0)
 
     def x_start(k):
         x_spread.wait_group(group(k), k)
@@ -677,13 +677,9 @@
 
     gg_total = jnp.zeros((n_dp, LANES), F32)
     x_gather.mid(0)
-    x_gather.mid(1)
-    x_gather.far(0)
     for k in range(GROUPS):
-        if k + 2 < GROUPS:
-            x_gather.mid(k + 2)
-        if k == 0:
-            x_gather.far(1)
+        if k + 1 < GROUPS:
+            x_gather.mid(k + 1)
         x_gather.end(k)
         gg_total = gg_total + expert_group(k)
         if k == GROUPS - 1:
@@ -691,12 +687,10 @@
             gg_exchange = Exchange(lambda peer: gg_all.at[e], lambda b: gg_all.at[b], gg_all)
             gg_exchange.start()
         reduces.append(
-            Reduce(group_first(k), Q, input_partial(group_first(k)), bufs, k if k < 2 else None)
+            Reduce(group_first(k), Q, input_partial(group_first(k)), bufs, None)
         )
         reduces[k].local()
         reduces[k].pairs()
-        if k in (1, 2):
-            reduces[k - 1].onward()
 
     def up_back(b, carry):
         rows = pl.ds(pl.multiple_of(b * F, F), F)

time: 124 us -> 116 us (0.935)
  Pallas kernels: 123 us -> 115 us
    pallas_call x1, Pallas kernels: 119 us -> 111 us  [body(): pl.pallas_call(functools.partial(layer_kernel, z), out_shape=(jax.ShapeDt...]
where the time goes in v4:
time: 116 us
  Pallas kernels  115 us (99%)
    pallas_call x1, Pallas kernels, body(): pl.pallas_call(functools.partial(layer_kernel, z), out_shape=(jax.ShapeDt...  111 us
    pallas_call x1, Pallas kernels, body(): pl.pallas_call(hand_on, out_shape=tuple((jax.ShapeDtypeStruct(r.shape, r....  3.95 us

profile of v4, /device:TPU:1, one launch (start us, length us, event | category | flops | bytes accessed | tf_op | source)
XLA Modules:
  0.0 116.0 jit_solution(15232142862232110406)
XLA Ops:
  0.6 111.2 %layer.1 = (bf16[128,256]{1,0:T(8,128)(2,1)}, bf16[2048,512]{1,0:T(8,128)(2,1)}, bf16[512,2048]{1,0:T(8,128)(2,1)}) custom-call(s32[4]{0:T(128)} %src_ref.1, s32[4]{0:T(128)} %slen_ref.1, s32[4]{0:T(128)} %tlen_ref.1, s32[4,2,32]{2,1,0:T(2,128)} %bitcast.20, f32[1,2048]{1,0:T(1,128)} %bitcast.18, f32[1,2048]{1,0:T(1,128)} %bitcast.19, ...), custom_call_target="tpu_custom_call" | custom-call | tf_op jit(solution)/shard_map/layer/pallas_call | solution.py:906
  111.8 4.0 %hand_on.1 = (bf16[128,256]{1,0:T(8,128)(2,1)}, bf16[2048,512]{1,0:T(8,128)(2,1)}, bf16[512,2048]{1,0:T(8,128)(2,1)}) custom-call(bf16[128,256]{1,0:T(8,128)(2,1)} %get-tuple-element.9.refs_0_, bf16[2048,512]{1,0:T(8,128)(2,1)} %get-tuple-element.10.refs_1_, bf16[512,2048]{1,0:T(8,128)(2,1)} %get-tuple-element.11.refs_2_), custom_call_target="tpu_custom_call" | custom-call | tf_op jit(solution)/shard_map/hand_on/pallas_call | solution.py:927
